TPU v7x, 32 devices: a whole 2x2x4 slice. The times are simulated.
32 devices in a mesh: ctx: 8 (over y, x, core), tp: 4 (over z).
Axes of the slice: x: 2, y: 2, z: 4, core: 2. Of those that a mesh axis runs over, the one named last changes fastest.
Arguments:
- x_gate: bfloat16 [1024, 2048], P('ctx', 'tp'), may hold values from -6 to 6
- x_post: bfloat16 [1024, 2048], P('ctx', 'tp'), may hold values from -6 to 6
- values: bfloat16 [1024, 2048], P('ctx', 'tp'), may hold values from -6 to 6
- decay: float32 [2, 2048, 16], P(None, 'tp'), may hold values from 0.00024414062 to 0.05
- residue: float32 [2, 2048, 16], P(None, 'tp'), may hold values from -4 to 4
- w_out: bfloat16 [2048, 2048], P(('tp', 'ctx')), may hold values from -0.125 to 0.125
Outputs:
- projected: bfloat16 [1024, 2048], P('ctx', 'tp')
All inputs are finite; a program needn't handle non-finite values.
Results may differ from a plain program's by a relative error of at most 0.015.
Values may be sent and summed in bfloat16 or wider, within the bound.
No kernel may reach another device: no remote copies, remote signals or barrier semaphores. Data moves between devices by JAX's collectives and lax.ppermute only.
A program may use at most 128 MiB of HBM per device.

v0:
```python
import functools
import math

import jax
import jax.numpy as jnp
from jax import lax
from jax.experimental import pallas as pl
from jax.experimental.pallas import tpu as pltpu
from jax.sharding import PartitionSpec as P

HIGHEST = lax.Precision.HIGHEST


def partner(value, axis, bit):
    mask = 2**bit
    pairs = [(source, source ^ mask) for source in range(lax.axis_size(axis))]
    return lax.ppermute(value, axis, pairs)


def radices(length_all):
    last_radix = min(128, length_all // 4)
    first_radix = min(32, length_all // last_radix)
    return (first_radix, length_all // (first_radix * last_radix), last_radix)


def rotation(row_count, col_count, modulus):
    product = (
        lax.broadcasted_iota(jnp.int32, (row_count, col_count), 0)
        * lax.broadcasted_iota(jnp.int32, (row_count, col_count), 1)
        % modulus
    )
    angle = product.astype(jnp.float32) * (2.0 * math.pi / modulus)
    return (jnp.cos(angle), -jnp.sin(angle))


def tables(radix_sizes):
    first_radix, mid_radix, last_radix = radix_sizes
    length_all = first_radix * mid_radix * last_radix
    outer_real, outer_imag = rotation(first_radix, first_radix, first_radix)
    mid_real, mid_imag = rotation(mid_radix, mid_radix, mid_radix)
    last_real, last_imag = rotation(last_radix, last_radix, last_radix)
    twist_real, twist_imag = rotation(first_radix, mid_radix * last_radix, length_all)
    twist_real = twist_real.reshape(first_radix, mid_radix, last_radix)
    twist_imag = twist_imag.reshape(first_radix, mid_radix, last_radix)
    inner_real, inner_imag = rotation(mid_radix, last_radix, mid_radix * last_radix)
    return (
        outer_real,
        outer_imag,
        mid_real,
        mid_imag,
        last_real,
        last_imag,
        twist_real,
        twist_imag,
        inner_real,
        inner_imag,
    )


def apply_matrix(pattern, real_part, imag_part, matrix_real, matrix_imag):
    out_real = jnp.einsum(pattern, real_part, matrix_real, precision=HIGHEST) - jnp.einsum(
        pattern, imag_part, matrix_imag, precision=HIGHEST
    )
    out_imag = jnp.einsum(pattern, real_part, matrix_imag, precision=HIGHEST) + jnp.einsum(
        pattern, imag_part, matrix_real, precision=HIGHEST
    )
    return (out_real, out_imag)


def complex_times(left_real, left_imag, right_real, right_imag):
    return (
        left_real * right_real - left_imag * right_imag,
        left_real * right_imag + left_imag * right_real,
    )


def forward(real_part, imag_part, table_set, radix_sizes):
    first_radix, mid_radix, last_radix = radix_sizes
    half_first = first_radix // 2
    batch_rows = real_part.shape[0]
    (
        outer_real,
        outer_imag,
        mid_real,
        mid_imag,
        last_real,
        last_imag,
        twist_real,
        twist_imag,
        inner_real,
        inner_imag,
    ) = table_set
    real_part = real_part.reshape(batch_rows, half_first, mid_radix, last_radix)
    imag_part = imag_part.reshape(batch_rows, half_first, mid_radix, last_radix)
    real_part, imag_part = apply_matrix(
        "banm,ak->bknm", real_part, imag_part, outer_real[:half_first], outer_imag[:half_first]
    )
    real_part, imag_part = complex_times(real_part, imag_part, twist_real, twist_imag)
    real_part, imag_part = apply_matrix("bknm,nj->bkjm", real_part, imag_part, mid_real, mid_imag)
    real_part, imag_part = complex_times(real_part, imag_part, inner_real, inner_imag)
    return apply_matrix("bkjm,mq->bkjq", real_part, imag_part, last_real, last_imag)


def inverse(real_part, imag_part, table_set, radix_sizes):
    first_radix, mid_radix, last_radix = radix_sizes
    half_first = first_radix // 2
    batch_rows = real_part.shape[0]
    (
        outer_real,
        outer_imag,
        mid_real,
        mid_imag,
        last_real,
        last_imag,
        twist_real,
        twist_imag,
        inner_real,
        inner_imag,
    ) = table_set
    real_part, imag_part = apply_matrix(
        "bkjq,mq->bkjm", real_part, imag_part, last_real / last_radix, -last_imag / last_radix
    )
    real_part, imag_part = complex_times(real_part, imag_part, inner_real, -inner_imag)
    real_part, imag_part = apply_matrix(
        "bkjm,nj->bknm", real_part, imag_part, mid_real / mid_radix, -mid_imag / mid_radix
    )
    real_part, imag_part = complex_times(real_part, imag_part, twist_real, -twist_imag)
    matrix_real = outer_real[:half_first] / first_radix
    matrix_imag = -outer_imag[:half_first] / first_radix
    out_real, out_imag = apply_matrix(
        "bknm,ak->banm", real_part, imag_part, matrix_real, matrix_imag
    )
    return (out_real.reshape(batch_rows, -1), out_imag.reshape(batch_rows, -1))


def spectrum(decay_rows, residue_rows, radix_sizes, seq_length):
    first_radix, mid_radix, last_radix = radix_sizes
    length_all = first_radix * mid_radix * last_radix
    poles = decay_rows.shape[1]
    shape_all = (first_radix, mid_radix, last_radix)
    frequency = (
        lax.broadcasted_iota(jnp.int32, shape_all, 0)
        + first_radix * lax.broadcasted_iota(jnp.int32, shape_all, 1)
        + first_radix * mid_radix * lax.broadcasted_iota(jnp.int32, shape_all, 2)
    )
    half_angle = frequency.astype(jnp.float32) * (math.pi / length_all)
    sin_half = jnp.sin(half_angle)
    sin_full = jnp.sin(2.0 * half_angle)
    parity_sign = (1 - 2 * (frequency % 2)).astype(jnp.float32)

    def add_pole(pole_index, running):
        run_real, run_imag = running
        rate_col = lax.dynamic_slice_in_dim(decay_rows, pole_index, 1, 1).reshape(-1, 1, 1, 1)
        weight = lax.dynamic_slice_in_dim(residue_rows, pole_index, 1, 1).reshape(
            -1, 1, 1, 1
        ) * jnp.sqrt(2.0 * rate_col / poles)
        retained = jnp.exp(-rate_col)
        den_real = -jnp.expm1(-rate_col) + 2.0 * retained * sin_half * sin_half
        den_imag = retained * sin_full
        pole_scale = (
            weight
            * (1.0 - jnp.exp(-rate_col * seq_length) * parity_sign)
            / (den_real * den_real + den_imag * den_imag)
        )
        return (run_real + pole_scale * den_real, run_imag - pole_scale * den_imag)

    zeros_all = jnp.zeros((decay_rows.shape[0],) + shape_all, jnp.float32)
    return lax.fori_loop(0, poles, add_pole, (zeros_all, zeros_all))


def general(x_gate, x_post, values, decay, residue, w_out):
    tok_rows, block_width = x_gate.shape
    ctx_count = lax.axis_size("ctx")
    tp_count = lax.axis_size("tp")
    chan_group = block_width // ctx_count
    seq_length = tok_rows * ctx_count
    radix_sizes = radices(2 * seq_length)
    table_set = tables(radix_sizes)
    first_row = lax.axis_index("ctx") * chan_group
    own_rate = lax.dynamic_slice_in_dim(decay, first_row, chan_group, 1)
    own_residue = lax.dynamic_slice_in_dim(residue, first_row, chan_group, 1)
    own_spec = [
        spectrum(own_rate[filter_index], own_residue[filter_index], radix_sizes, seq_length)
        for filter_index in range(2)
    ]
    forward_rows = [x_gate, values] + [x_post]
    row_count = len(forward_rows)
    base_rows = jnp.stack(forward_rows)
    copied = base_rows
    for bit_index in range(tp_count.bit_length() - 1):
        copied = partner(copied, "tp", bit_index)
    sent_rows = jnp.concatenate([base_rows, copied[:, :, ::-1]], axis=0)
    received = lax.all_to_all(
        jnp.swapaxes(sent_rows, 1, 2), "ctx", split_axis=1, concat_axis=2, tiled=True
    )
    gate_fwd = received[0].astype(jnp.float32)
    value_fwd = received[1].astype(jnp.float32)
    mirrored = received[row_count:, :, ::-1].astype(jnp.float32)
    spec_real, spec_imag = forward(value_fwd, mirrored[1], table_set, radix_sizes)
    spec_real, spec_imag = complex_times(spec_real, spec_imag, own_spec[0][0], own_spec[0][1])
    along_fwd, along_rev = inverse(spec_real, spec_imag, table_set, radix_sizes)
    spec_real, spec_imag = forward(
        gate_fwd * along_fwd, mirrored[0] * along_rev, table_set, radix_sizes
    )
    spec_real, spec_imag = complex_times(spec_real, spec_imag, own_spec[1][0], own_spec[1][1])
    sum_fwd, sum_rev = inverse(spec_real, spec_imag, table_set, radix_sizes)
    sum_fwd = received[2].astype(jnp.float32) * sum_fwd
    sum_rev = mirrored[2] * sum_rev
    results = jnp.stack([sum_fwd, sum_rev[:, ::-1]])
    returned = lax.all_to_all(
        results.astype(jnp.bfloat16), "ctx", split_axis=2, concat_axis=1, tiled=True
    ).astype(results.dtype)
    flipped = returned[1, ::-1, :]
    for bit_index in range(tp_count.bit_length() - 1):
        flipped = partner(flipped.astype(jnp.bfloat16), "tp", bit_index).astype(flipped.dtype)
    total_rows = returned[0] + flipped
    total_rows = total_rows.T
    mixed_rows = total_rows.astype(jnp.bfloat16)
    whole_rows = lax.all_gather(mixed_rows, "tp", axis=1, tiled=True)
    projected = lax.dot_general(
        whole_rows,
        lax.all_gather(w_out, "ctx", axis=0, tiled=True),
        (((1,), (1,)), ((), ())),
        preferred_element_type=jnp.float32,
    )
    return projected.astype(jnp.bfloat16)


def cycle(row_factor, col_factor, modulus):
    angle = (row_factor * col_factor % modulus).astype(jnp.float32) * (2.0 * math.pi / modulus)
    return jnp.cos(angle), jnp.sin(angle)


def put_tables(table_ref, back_ref):
    block = table_ref.shape[1]
    modulus = 4 * block
    coarse = 16
    rows = lax.broadcasted_iota(jnp.int32, (coarse, block), 0)
    cols = lax.broadcasted_iota(jnp.int32, (coarse, block), 1)

    def parts(big, small):
        for place in range(block // coarse):
            big_cos, big_sin = (part[place : place + 1] for part in big)
            span = slice(place * coarse, (place + 1) * coarse)
            below = slice(block + place * coarse, block + (place + 1) * coarse)
            cos = halves(big_cos * small[0] - big_sin * small[1])
            sin = halves(-(big_sin * small[0] + big_cos * small[1]))
            yield span, below, cos, sin

    frequency = 2 * cols + 1
    for span, _, cos, sin in parts(cycle(coarse * rows, frequency, modulus), cycle(rows, frequency, modulus)):
        table_ref[0, span, :block], table_ref[1, span, :block] = cos
        table_ref[0, span, block:], table_ref[1, span, block:] = sin
    for span, below, cos, sin in parts(cycle(2 * coarse * rows, cols, modulus), cycle(2 * rows + 1, cols, modulus)):
        back_ref[0, span], back_ref[1, span] = cos
        back_ref[0, below], back_ref[1, below] = sin


def halves(value):
    high = value.astype(jnp.bfloat16)
    return high, (value - high.astype(jnp.float32)).astype(jnp.bfloat16)


def mul(left, right):
    return jnp.dot(left, right, preferred_element_type=jnp.float32)


def mul3(high, low, table_ref):
    return mul(high, table_ref[0]) + (mul(low, table_ref[0]) + mul(high, table_ref[1]))


def pack_kernel(
    gate_hbm, value_hbm, post_hbm, decay_hbm, residue_hbm,
    out_hbm, own_hbm, sent_hbm, held_ref, cut_ref, ready_ref, sems, out_sems,
):
    ctx_count, _, group, tok = out_hbm.shape
    width = gate_hbm.shape[1]
    half = decay_hbm.shape[0]
    position = lax.axis_index("ctx")
    pairs = []
    for place, index in enumerate((position, ctx_count - 1 - position)):
        columns = pl.ds(pl.multiple_of(index * group // tok * tok, tok), tok)
        pairs += [(decay_hbm.at[:, columns], cut_ref.at[place, :half]), (residue_hbm.at[:, columns], cut_ref.at[place, half:])]
    pairs += [(source, held_ref.at[place]) for place, source in enumerate((value_hbm, gate_hbm, post_hbm))]
    copies = [pltpu.make_async_copy(*pair, sems.at[place]) for place, pair in enumerate(pairs)]
    for copy in copies:
        copy.start()
    sends = []
    for place, target in enumerate((own_hbm, sent_hbm)):
        copies[2 * place].wait()
        copies[2 * place + 1].wait()
        sends.append(pltpu.make_async_copy(cut_ref.at[place], target, out_sems.at[3 + place]))
        sends[-1].start()
    for place, copy in enumerate(copies[4:]):
        copy.wait()
        for first in range(0, width, tok):
            turned = held_ref[place, :, first : first + tok].T
            for part in range(tok // group):
                ready_ref[first // group + part, place] = turned[part * group : (part + 1) * group]
        sends.append(pltpu.make_async_copy(ready_ref.at[:, place], out_hbm.at[:, place], out_sems.at[place]))
        sends[-1].start()
    for send in sends:
        send.wait()


def mirror_rows(value):
    row = lax.broadcasted_iota(jnp.int32, (8, value.shape[1]), 0)
    result = []
    for first in range(value.shape[0] - 8, -1, -8):
        part = value[first : first + 8]
        for shift in (1, 2, 4):
            part = jnp.where(row & shift == 0, pltpu.roll(part, 8 - shift, 0), pltpu.roll(part, shift, 0))
        result.append(part)
    return jnp.concatenate(result, axis=0)


def put_spectra(poles, index, turned, out_ref, time_ref, table_ref):
    blocks, group, twice = out_ref.shape
    block = twice // 2
    lanes = 128
    ramp = lax.broadcasted_iota(jnp.int32, (8, lanes), 1).astype(jnp.float32)
    sign = (1 - 2 * (lax.broadcasted_iota(jnp.int32, (group, block), 1) % 2)).astype(jnp.float32)
    for row in range(0, group, 8):
        rows = slice(row, row + 8)
        rate = turned[rows, index * poles : (index + 1) * poles]
        scale = turned[rows, (2 + index) * poles : (3 + index) * poles] * (jnp.sqrt(rate * (2.0 / poles)) / block)
        slope = rate * -math.log2(math.e)
        jump = jnp.exp2(slope * lanes)
        sums = [None] * (blocks * block // lanes)
        for pole in range(poles):
            term = scale[:, pole : pole + 1] * jnp.exp2(slope[:, pole : pole + 1] * ramp)
            step = jnp.broadcast_to(jump[:, pole : pole + 1], (8, lanes))
            for place in range(len(sums)):
                sums[place] = term if pole == 0 else sums[place] + term
                if place + 1 < len(sums):
                    term = term * step
        for place, total in enumerate(sums):
            lag, lane = divmod(place * lanes, block)
            time_ref[lag * group + row : lag * group + row + 8, lane : lane + lanes] = total
    spec = mul3(*halves(time_ref[...]), table_ref)
    for lag in range(blocks):
        real = spec[lag * group : (lag + 1) * group, :block]
        imag = spec[lag * group : (lag + 1) * group, block:]
        if lag > 0:
            real = real - sign * spec[(lag - 1) * group : lag * group, block:]
            imag = imag + sign * spec[(lag - 1) * group : lag * group, :block]
        out_ref[lag, :, :block] = real
        out_ref[lag, :, block:] = imag


def filter_kernel(poles, par_ref, out_ref, table_ref, back_ref, time_ref, turned_ref):
    group = out_ref.shape[2]
    put_tables(table_ref, back_ref)
    turned_ref[...] = par_ref[...].T
    turned = turned_ref[pl.ds(pl.multiple_of(lax.axis_index("ctx") * group % turned_ref.shape[0], group), group)]
    for index in range(2):
        put_spectra(poles, index, turned, out_ref.at[index], time_ref.at[index], table_ref)


def conv_kernel(
    poles, x_ref, own_ref, par_ref, table_ref, back_ref, out_hbm,
    paired_ref, time_ref, turned_ref, spec_ref, high_ref, ready_ref, sems,
):
    turned_ref[...] = par_ref[...].T
    blocks, group, twice = own_ref.shape[1:]
    block = twice // 2
    rows_all = blocks * group
    tall, wide = 16, 128
    pieces = x_ref.shape[0] // blocks
    first = (x_ref.shape[0] - 1 - lax.axis_index("ctx")) * group % turned_ref.shape[0]
    turned = mirror_rows(turned_ref[pl.ds(pl.multiple_of(first, group), group)])

    def rows_of(position):
        return jnp.concatenate(
            [
                jnp.concatenate([x_ref[m * pieces + s, position] for s in range(pieces)], axis=1)
                for m in range(blocks)
            ],
            axis=0,
        )

    def times(index, side, source, row, lane):
        data = []
        for m in range(blocks):
            rows = slice(source + m * group + row, source + m * group + row + tall)
            data.append((spec_ref[rows, lane : lane + wide], spec_ref[rows, block + lane : block + lane + wide]))
        sums = [None] * blocks
        for lag in range(blocks):
            h_ref = (own_ref, paired_ref)[side]
            f_re = h_ref[index, lag, row : row + tall, lane : lane + wide]
            f_im = h_ref[index, lag, row : row + tall, block + lane : block + lane + wide]
            for m in range(blocks - lag):
                target, (d_re, d_im) = (m + lag, data[m]) if side == 0 else (m, data[m + lag])
                if side == 0:
                    real, imag = f_re * d_re - f_im * d_im, f_re * d_im + f_im * d_re
                else:
                    real, imag = f_re * d_re + f_im * d_im, f_re * d_im - f_im * d_re
                if sums[target] is not None:
                    real, imag = sums[target][0] + real, sums[target][1] + imag
                sums[target] = (real, imag)
        return sums

    def to_time(rows):
        return mul(high_ref[rows], back_ref[0]) + mul(high_ref[rows], back_ref[1])

    def keep(target, row, lane, sums):
        for m in range(blocks):
            rows = slice(target + m * group + row, target + m * group + row + tall)
            for part in range(2):
                cols = slice(part * block + lane, part * block + lane + wide)
                high_ref[rows, cols] = sums[m][part].astype(jnp.bfloat16)

    chunks = [(row, lane) for row in range(0, group, tall) for lane in range(0, block, wide)]

    value = rows_of(0)
    gate = rows_of(1).astype(jnp.float32)
    spec_ref[:rows_all] = mul(value, table_ref[0]) + mul(value, table_ref[1])
    sides = [slice(side * rows_all, (side + 1) * rows_all) for side in range(2)]
    gated = []
    put_spectra(poles, 0, turned, paired_ref.at[0], time_ref.at[0], table_ref)
    for side in range(2):
        for row, lane in chunks:
            keep(side * rows_all, row, lane, times(0, side, 0, row, lane))
        gated.append(halves(gate * to_time(sides[side])))
    put_spectra(poles, 1, turned, paired_ref.at[1], time_ref.at[1], table_ref)
    for side in range(2):
        spec_ref[sides[side]] = mul3(*gated[side], table_ref)
    for row, lane in chunks:
        ahead, back = times(1, 0, 0, row, lane), times(1, 1, rows_all, row, lane)
        keep(0, row, lane, [(a[0] + b[0], a[1] + b[1]) for a, b in zip(ahead, back)])
    post = rows_of(2)
    tok = block // pieces
    sends = []
    for part in range(2):
        rows = slice(part * rows_all // 2, (part + 1) * rows_all // 2)
        summed = to_time(rows)
        mixed = (post[rows].astype(jnp.float32) * summed).astype(jnp.bfloat16)
        first = part * blocks // 2 * pieces
        for m in range(blocks // 2):
            for s in range(pieces):
                ready_ref[first + m * pieces + s] = mixed[m * group : (m + 1) * group, s * tok : (s + 1) * tok]
        span = pl.ds(first, blocks // 2 * pieces)
        for copy in range(out_hbm.shape[0]):
            sends.append(pltpu.make_async_copy(ready_ref.at[span], out_hbm.at[copy, span], sems.at[part, copy]))
            sends[-1].start()
    for send in sends:
        send.wait()


def project_kernel(mixed_ref, *refs):
    w_refs, (out_hbm, held_ref, ready_ref, sems) = refs[:-4], refs[-4:]
    rows = w_refs[0].shape[0]
    tile = 2 * rows
    position = lax.axis_index("ctx")
    even = pl.multiple_of(position % 2 * rows, rows)
    odd = pl.multiple_of((1 - position % 2) * rows, rows)
    sends = []
    for half, half_refs in enumerate((w_refs[:4], w_refs[4:])):
        total = mul(jnp.concatenate([w_ref[...] for w_ref in half_refs], axis=0), mixed_ref[...])
        for pair in range(2):
            place = 2 * half + pair
            held_ref[place, pl.ds(even, rows)] = total[pair * tile : pair * tile + rows]
            held_ref[place, pl.ds(odd, rows)] = total[pair * tile + rows : (pair + 1) * tile]
            ready_ref[place] = held_ref[place].T.astype(jnp.bfloat16)
            columns = pl.ds(pl.multiple_of((position // 2 ^ place) * tile, tile), tile)
            sends.append(pltpu.make_async_copy(ready_ref.at[place], out_hbm.at[:, columns], sems.at[place]))
            sends[-1].start()
    for send in sends:
        send.wait()


def whole_call(kernel, out_shape, scratch, flops, nbytes, *operands, in_hbm=0, out_hbm=()):
    results = pl.pallas_call(
        kernel,
        out_shape=out_shape,
        in_specs=[
            pl.BlockSpec(memory_space=pltpu.HBM if place < in_hbm else pltpu.VMEM) for place in range(len(operands))
        ],
        out_specs=[
            pl.BlockSpec(memory_space=pltpu.HBM if place in out_hbm else pltpu.VMEM) for place in range(len(out_shape))
        ],
        scratch_shapes=scratch,
        cost_estimate=pl.CostEstimate(flops=flops, bytes_accessed=nbytes, transcendentals=0),
        compiler_params=pltpu.CompilerParams(vmem_limit_bytes=None if in_hbm else 32 * 2**20),
    )(*operands)
    return results if len(out_shape) > 1 else results[0]


def blocked(x_gate, x_post, values, decay, residue, w_out):
    tok, width = x_gate.shape
    ctx_count = lax.axis_size("ctx")
    tp_count = lax.axis_size("tp")
    group = width // ctx_count
    poles = decay.shape[2]
    block = 2 * tok
    blocks = tok * ctx_count // block
    rows, channels = w_out.shape
    half = 2 * poles

    packed, own, mirrored = whole_call(
        pack_kernel,
        (
            jax.ShapeDtypeStruct((ctx_count, 3, group, tok), jnp.bfloat16),
            jax.ShapeDtypeStruct((2 * half, tok), jnp.float32),
            jax.ShapeDtypeStruct((2 * half, tok), jnp.float32),
        ),
        [
            pltpu.VMEM((3, tok, width), jnp.bfloat16),
            pltpu.VMEM((2, 2 * half, tok), jnp.float32),
            pltpu.VMEM((ctx_count, 3, group, tok), jnp.bfloat16),
            pltpu.SemaphoreType.DMA((7,)),
            pltpu.SemaphoreType.DMA((5,)),
        ],
        0,
        6 * tok * width * 2,
        x_gate,
        values,
        x_post,
        jnp.swapaxes(decay, 1, 2).reshape(half, width),
        jnp.swapaxes(residue, 1, 2).reshape(half, width),
        in_hbm=5,
        out_hbm=(0, 1, 2),
    )
    paired = lax.ppermute(mirrored, "tp", [(z, tp_count - 1 - z) for z in range(tp_count)])
    received = lax.all_to_all(packed, "ctx", split_axis=0, concat_axis=0, tiled=True)

    w_late, mirrored = lax.optimization_barrier((w_out, mirrored))
    w_x, w_y = partner(w_late, "ctx", 1), partner(w_late, "ctx", 2)
    own_spectra, table, back_table = whole_call(
        functools.partial(filter_kernel, poles),
        (
            jax.ShapeDtypeStruct((2, blocks, group, 2 * block), jnp.float32),
            jax.ShapeDtypeStruct((2, block, 2 * block), jnp.bfloat16),
            jax.ShapeDtypeStruct((2, 2 * block, block), jnp.bfloat16),
        ),
        [
            pltpu.VMEM((2, blocks * group, block), jnp.float32),
            pltpu.VMEM((tok, 2 * half), jnp.float32),
        ],
        2 * 2 * blocks * group * block * 2 * block * 3,
        2 * blocks * group * 2 * block * 4,
        own,
    )
    mixed = whole_call(
        functools.partial(conv_kernel, poles),
        (jax.ShapeDtypeStruct((tp_count, ctx_count, group, tok), jnp.bfloat16),),
        [
            pltpu.VMEM((2, blocks, group, 2 * block), jnp.float32),
            pltpu.VMEM((2, blocks * group, block), jnp.float32),
            pltpu.VMEM((tok, 2 * half), jnp.float32),
            pltpu.VMEM((2 * blocks * group, 2 * block), jnp.float32),
            pltpu.VMEM((2 * blocks * group, 2 * block), jnp.bfloat16),
            pltpu.VMEM((ctx_count, group, tok), jnp.bfloat16),
            pltpu.SemaphoreType.DMA((2, tp_count)),
        ],
        2 * 8 * blocks * group * block * 2 * block * 3,
        4 * blocks * group * 2 * block * 4,
        received,
        own_spectra,
        paired,
        table,
        back_table,
        out_hbm=(0,),
    )
    mixed, w_x, w_y, w_own = lax.optimization_barrier((mixed, w_x, w_y, w_out))
    lower = rows // 2
    w_far = [partner(w_x[:lower], "ctx", 2), partner(w_y[lower:], "ctx", 1)]
    w_blocks = []
    for block in (w_own, w_x, w_y):
        w_blocks += [block, partner(block, "ctx", 0)]
    w_blocks += w_far + [partner(block, "ctx", 0) for block in w_far]
    every = lax.all_to_all(
        mixed.reshape(tp_count * ctx_count, group, tok), ("tp", "ctx"), split_axis=0, concat_axis=0, tiled=True
    ).reshape(channels, tok)
    return whole_call(
        project_kernel,
        (jax.ShapeDtypeStruct((tok, rows * ctx_count), jnp.bfloat16),),
        [
            pltpu.VMEM((ctx_count // 2, 2 * rows, tok), jnp.float32),
            pltpu.VMEM((ctx_count // 2, tok, 2 * rows), jnp.bfloat16),
            pltpu.SemaphoreType.DMA((ctx_count // 2,)),
        ],
        2 * tok * rows * ctx_count * channels,
        2 * rows * ctx_count * channels,
        every,
        *w_blocks,
        out_hbm=(0,),
    )


def local(x_gate, x_post, values, decay, residue, w_out):
    tok, width = x_gate.shape
    ctx_count = lax.axis_size("ctx")
    if tok == 128 and width == 512 and ctx_count == 8 and w_out.shape[0] == 64 and lax.axis_size("tp") == 4:
        return blocked(x_gate, x_post, values, decay, residue, w_out)
    return general(x_gate, x_post, values, decay, residue, w_out)


def solution(mesh):
    in_specs = (
        P("ctx", "tp"),
        P("ctx", "tp"),
        P("ctx", "tp"),
        P(None, "tp", None),
        P(None, "tp", None),
        P(("tp", "ctx"), None),
    )
    out_specs = P("ctx", "tp")
    return jax.shard_map(local, mesh=mesh, in_specs=in_specs, out_specs=out_specs, check_vma=False)
```

profile of v0, /device:TPU:1, one launch (start us, length us, event | category | flops | bytes accessed | tf_op | source)
XLA Modules:
  0.0 41.8 jit_solution(894262129727637028)
XLA Ops:
  0.0 2.0 %shard_map.64 = (bf16[8,3,64,128]{3,2,1,0:T(8,128)(2,1)}, f32[64,128]{1,0:T(8,128)}, f32[64,128]{1,0:T(8,128)}) custom-call(bf16[128,512]{1,0:T(8,128)(2,1)} %gate_hbm.1, bf16[128,512]{1,0:T(8,128)(2,1)} %value_hbm.1, bf16[128,512]{1,0:T(8,128)(2,1)} %post_hbm.1, f32[32,512]{1,0:T(8,128)} %bitcast.9, f32[32,512]{1,0:T(8,128)} %bitcast.10), custom_call_target="tpu_custom_call" | custom-call | bytes 786432 | tf_op jit(solution)/shard_map/pallas_call | solution.py:473
  2.0 0.0 copy-start
  2.0 0.0 copy-start.2
  2.0 0.0 copy-start.1
  2.0 5.4 %all-to-all-start = ((bf16[8,3,64,128]{3,2,1,0:T(8,128)(2,1)}), bf16[8,3,64,128]{3,2,1,0:T(8,128)(2,1)S(1)}, u32[]{:S(2)}, u32[]{:S(2)}) async-start(bf16[8,3,64,128]{3,2,1,0:T(8,128)(2,1)} %get-tuple-element.16), calls=%async_computation | async-start | bytes 786432 | tf_op jit(solution)/shard_map/all_to_all | solution.py:525
  7.4 0.0 copy-done
  7.4 1.4 %collective-permute-start.1 = (bf16[64,2048]{1,0:T(8,128)(2,1)S(1)}, bf16[64,2048]{1,0:T(8,128)(2,1)S(1)}, u32[]{:S(2)}, u32[]{:S(2)}) collective-permute-start(bf16[64,2048]{1,0:T(8,128)(2,1)S(1)} %copy-done), channel_id=1, source_target_pairs={{0,8},{4,12},{8,0},{12,4},{16,24},{20,28},{24,16},{28,20},{1,9},{5... | collective-permute-start | bytes 786440 | tf_op jit(solution)/shard_map/ppermute | solution.py:17
  8.8 1.2 %collective-permute-start.2 = (bf16[64,2048]{1,0:T(8,128)(2,1)S(1)}, bf16[64,2048]{1,0:T(8,128)(2,1)S(1)}, u32[]{:S(2)}, u32[]{:S(2)}) collective-permute-start(bf16[64,2048]{1,0:T(8,128)(2,1)S(1)} %copy-done), channel_id=1, source_target_pairs={{0,16},{4,20},{8,24},{12,28},{16,0},{20,4},{24,8},{28,12},{1,17},{... | collective-permute-start | bytes 786440 | tf_op jit(solution)/shard_map/ppermute | solution.py:17
  10.0 0.0 copy-done.2
  10.0 3.3 %collective-permute-start = (f32[64,128]{1,0:T(8,128)S(1)}, f32[64,128]{1,0:T(8,128)S(1)}, u32[]{:S(2)}, u32[]{:S(2)}) collective-permute-start(f32[64,128]{1,0:T(8,128)S(1)} %copy-done.2), channel_id=1, source_target_pairs={{0,3},{1,2},{2,1},{3,0},{4,7},{5,6},{6,5},{7,4},{8,11},{9,10},{10,... | collective-permute-start | bytes 98312 | tf_op jit(solution)/shard_map/ppermute | solution.py:524
  13.3 0.0 copy-done.1
  13.3 2.5 %shard_map.65 = (f32[2,4,64,512]{3,2,1,0:T(8,128)S(1)}, bf16[2,256,512]{2,1,0:T(8,128)(2,1)S(1)}, bf16[2,512,256]{2,1,0:T(8,128)(2,1)S(1)}) custom-call(f32[64,128]{1,0:T(8,128)S(1)} %copy-done.1), custom_call_target="tpu_custom_call" | custom-call | flops 402653184 | bytes 1048576 | tf_op jit(solution)/shard_map/pallas_call | solution.py:473
  15.8 0.0 collective-permute-done.par_ref
  15.8 0.0 all-to-all-done.x_ref
  15.8 4.0 %shard_map.66 = bf16[4,8,64,128]{3,2,1,0:T(8,128)(2,1)} custom-call(bf16[8,3,64,128]{3,2,1,0:T(8,128)(2,1)S(1)} %all-to-all-done.x_ref, f32[2,4,64,512]{3,2,1,0:T(8,128)S(1)} %get-tuple-element.18.own_ref, f32[64,128]{1,0:T(8,128)S(1)} %collective-permute-done.par_ref, bf16[2,256,512]{2,1,0:T(8,128)(2,1)S(1)} %get-tuple-element.20.table_ref, ...), custom_call_target="tpu_custom_call" | custom-call | flops 1610612736 | bytes 2097152 | tf_op jit(solution)/shard_map/pallas_call | solution.py:473
  19.8 0.0 collective-permute-done.1.refs_2_
  19.8 0.0 collective-permute-done.2.refs_4_
  19.8 5.2 %all-to-all-start.1 = ((bf16[32,64,128]{2,1,0:T(8,128)(2,1)}), bf16[32,64,128]{2,1,0:T(8,128)(2,1)S(1)}, u32[]{:S(2)}, u32[]{:S(2)}) async-start(bf16[32,64,128]{2,1,0:T(8,128)(2,1)} %bitcast.4), calls=%async_computation.1 | async-start | bytes 1048576 | tf_op jit(solution)/shard_map/all_to_all | solution.py:572
  25.1 0.3 collective-permute-start.4
  25.5 0.3 collective-permute-start.5
  25.8 1.4 %collective-permute-start.6 = (bf16[32,2048]{1,0:T(8,128)(2,1)S(1)}, bf16[32,2048]{1,0:T(8,128)(2,1)S(1)}, u32[]{:S(2)}, u32[]{:S(2)}) collective-permute-start(bf16[32,2048]{1,0:T(8,128)(2,1)S(1)} %slice.6), channel_id=1, source_target_pairs={{0,16},{4,20},{8,24},{12,28},{16,0},{20,4},{24,8},{28,12},{1,17},{... | collective-permute-start | bytes 393224 | tf_op jit(solution)/shard_map/ppermute | solution.py:17
  27.2 0.6 %collective-permute-start.3 = (bf16[64,2048]{1,0:T(8,128)(2,1)S(1)}, bf16[64,2048]{1,0:T(8,128)(2,1)S(1)}, u32[]{:S(2)}, u32[]{:S(2)}) collective-permute-start(bf16[64,2048]{1,0:T(8,128)(2,1)S(1)} %copy-done), channel_id=1, source_target_pairs={{0,4},{4,0},{8,12},{12,8},{16,20},{20,16},{24,28},{28,24},{1,5},{5... | collective-permute-start | bytes 786440 | tf_op jit(solution)/shard_map/ppermute | solution.py:17
  27.8 1.2 %collective-permute-start.7 = (bf16[32,2048]{1,0:T(8,128)(2,1)S(1)}, bf16[32,2048]{1,0:T(8,128)(2,1)S(1)}, u32[]{:S(2)}, u32[]{:S(2)}) collective-permute-start(bf16[32,2048]{1,0:T(8,128)(2,1)S(1)} %slice.7), channel_id=1, source_target_pairs={{0,8},{4,12},{8,0},{12,4},{16,24},{20,28},{24,16},{28,20},{1,9},{5... | collective-permute-start | bytes 393224 | tf_op jit(solution)/shard_map/ppermute | solution.py:17
  29.0 5.6 %collective-permute-done.6.refs_6_ = bf16[32,2048]{1,0:T(8,128)(2,1)S(1)} collective-permute-done((bf16[32,2048]{1,0:T(8,128)(2,1)S(1)}, bf16[32,2048]{1,0:T(8,128)(2,1)S(1)}, u32[]{:S(2)}, u32[]{:S(2)}) %collective-permute-start.6) | collective-permute-done | bytes 131104 | tf_op jit(solution)/shard_map/ppermute | solution.py:17
  34.6 0.7 %collective-permute-start.8 = (bf16[32,2048]{1,0:T(8,128)(2,1)S(1)}, bf16[32,2048]{1,0:T(8,128)(2,1)S(1)}, u32[]{:S(2)}, u32[]{:S(2)}) collective-permute-start(bf16[32,2048]{1,0:T(8,128)(2,1)S(1)} %collective-permute-done.6.refs_6_), channel_id=1, source_target_pairs={{0,4},{4,0},{8,12},{12,8},{16,20},{20,16},{24,28},{28,24},{1,5},{5... | collective-permute-start | bytes 393224 | tf_op jit(solution)/shard_map/ppermute | solution.py:17
  35.3 0.0 collective-permute-done.7.refs_7_
  35.3 1.0 %collective-permute-start.9 = (bf16[32,2048]{1,0:T(8,128)(2,1)S(1)}, bf16[32,2048]{1,0:T(8,128)(2,1)S(1)}, u32[]{:S(2)}, u32[]{:S(2)}) collective-permute-start(bf16[32,2048]{1,0:T(8,128)(2,1)S(1)} %collective-permute-done.7.refs_7_), channel_id=1, source_target_pairs={{0,4},{4,0},{8,12},{12,8},{16,20},{20,16},{24,28},{28,24},{1,5},{5... | collective-permute-start | bytes 393224 | tf_op jit(solution)/shard_map/ppermute | solution.py:17
  36.2 0.0 collective-permute-done.4.refs_3_
  36.2 0.0 collective-permute-done.5.refs_5_
  36.2 0.0 collective-permute-done.3.refs_1_
  36.2 0.0 collective-permute-done.8.refs_8_
  36.2 1.0 %collective-permute-done.9.refs_9_ = bf16[32,2048]{1,0:T(8,128)(2,1)S(1)} collective-permute-done((bf16[32,2048]{1,0:T(8,128)(2,1)S(1)}, bf16[32,2048]{1,0:T(8,128)(2,1)S(1)}, u32[]{:S(2)}, u32[]{:S(2)}) %collective-permute-start.9) | collective-permute-done | bytes 131104 | tf_op jit(solution)/shard_map/ppermute | solution.py:17
  37.2 3.1 %all-to-all-done.1 = bf16[32,64,128]{2,1,0:T(8,128)(2,1)S(1)} async-done(((bf16[32,64,128]{2,1,0:T(8,128)(2,1)}), bf16[32,64,128]{2,1,0:T(8,128)(2,1)S(1)}, u32[]{:S(2)}, u32[]{:S(2)}) %all-to-all-start.1) | async-done | bytes 524320 | tf_op jit(solution)/shard_map/all_to_all | solution.py:572
  40.3 1.5 %shard_map.67 = bf16[128,512]{1,0:T(8,128)(2,1)} custom-call(bf16[2048,128]{1,0:T(8,128)(2,1)S(1)} %bitcast.8, bf16[64,2048]{1,0:T(8,128)(2,1)S(1)} %copy-done, bf16[64,2048]{1,0:T(8,128)(2,1)S(1)} %collective-permute-done.3.refs_1_, bf16[64,2048]{1,0:T(8,128)(2,1)S(1)} %collective-permute-done.1.refs_2_, ...), custom_call_target="tpu_custom_call" | custom-call | flops 268435456 | bytes 2097152 | tf_op jit(solution)/shard_map/pallas_call | solution.py:473
  (2 shorter events, 0.0 us)
Async XLA Ops:
  2.0 5.4 %copy-start = (bf16[64,2048]{1,0:T(8,128)(2,1)S(1)}, bf16[64,2048]{1,0:T(8,128)(2,1)}, u32[]{:S(2)}) copy-start(bf16[64,2048]{1,0:T(8,128)(2,1)} %refs_0_) | copy-start | bytes 786436
  2.0 8.0 %copy-start.2 = (f32[64,128]{1,0:T(8,128)S(1)}, f32[64,128]{1,0:T(8,128)}, u32[]{:S(2)}) copy-start(f32[64,128]{1,0:T(8,128)} %get-tuple-element.19) | copy-start | bytes 98308
  2.0 11.3 %copy-start.1 = (f32[64,128]{1,0:T(8,128)S(1)}, f32[64,128]{1,0:T(8,128)}, u32[]{:S(2)}) copy-start(f32[64,128]{1,0:T(8,128)} %get-tuple-element.17.par_ref) | copy-start | bytes 98308
  2.0 13.8 %all-to-all-start = ((bf16[8,3,64,128]{3,2,1,0:T(8,128)(2,1)}), bf16[8,3,64,128]{3,2,1,0:T(8,128)(2,1)S(1)}, u32[]{:S(2)}, u32[]{:S(2)}) async-start(bf16[8,3,64,128]{3,2,1,0:T(8,128)(2,1)} %get-tuple-element.16), calls=%async_computation | async-start | bytes 786432 | tf_op jit(solution)/shard_map/all_to_all | solution.py:525
  7.4 12.4 %collective-permute-start.1 = (bf16[64,2048]{1,0:T(8,128)(2,1)S(1)}, bf16[64,2048]{1,0:T(8,128)(2,1)S(1)}, u32[]{:S(2)}, u32[]{:S(2)}) collective-permute-start(bf16[64,2048]{1,0:T(8,128)(2,1)S(1)} %copy-done), channel_id=1, source_target_pairs={{0,8},{4,12},{8,0},{12,4},{16,24},{20,28},{24,16},{28,20},{1,9},{5... | collective-permute-start | bytes 786440 | tf_op jit(solution)/shard_map/ppermute | solution.py:17
  8.8 11.0 %collective-permute-start.2 = (bf16[64,2048]{1,0:T(8,128)(2,1)S(1)}, bf16[64,2048]{1,0:T(8,128)(2,1)S(1)}, u32[]{:S(2)}, u32[]{:S(2)}) collective-permute-start(bf16[64,2048]{1,0:T(8,128)(2,1)S(1)} %copy-done), channel_id=1, source_target_pairs={{0,16},{4,20},{8,24},{12,28},{16,0},{20,4},{24,8},{28,12},{1,17},{... | collective-permute-start | bytes 786440 | tf_op jit(solution)/shard_map/ppermute | solution.py:17
  10.0 5.8 %collective-permute-start = (f32[64,128]{1,0:T(8,128)S(1)}, f32[64,128]{1,0:T(8,128)S(1)}, u32[]{:S(2)}, u32[]{:S(2)}) collective-permute-start(f32[64,128]{1,0:T(8,128)S(1)} %copy-done.2), channel_id=1, source_target_pairs={{0,3},{1,2},{2,1},{3,0},{4,7},{5,6},{6,5},{7,4},{8,11},{9,10},{10,... | collective-permute-start | bytes 98312 | tf_op jit(solution)/shard_map/ppermute | solution.py:524
  19.8 20.4 %all-to-all-start.1 = ((bf16[32,64,128]{2,1,0:T(8,128)(2,1)}), bf16[32,64,128]{2,1,0:T(8,128)(2,1)S(1)}, u32[]{:S(2)}, u32[]{:S(2)}) async-start(bf16[32,64,128]{2,1,0:T(8,128)(2,1)} %bitcast.4), calls=%async_computation.1 | async-start | bytes 1048576 | tf_op jit(solution)/shard_map/all_to_all | solution.py:572
  25.1 11.1 %collective-permute-start.4 = (bf16[64,2048]{1,0:T(8,128)(2,1)S(1)}, bf16[64,2048]{1,0:T(8,128)(2,1)S(1)}, u32[]{:S(2)}, u32[]{:S(2)}) collective-permute-start(bf16[64,2048]{1,0:T(8,128)(2,1)S(1)} %collective-permute-done.1.refs_2_), channel_id=1, source_target_pairs={{0,4},{4,0},{8,12},{12,8},{16,20},{20,16},{24,28},{28,24},{1,5},{5... | collective-permute-start | bytes 786440 | tf_op jit(solution)/shard_map/ppermute | solution.py:17
  25.5 10.8 %collective-permute-start.5 = (bf16[64,2048]{1,0:T(8,128)(2,1)S(1)}, bf16[64,2048]{1,0:T(8,128)(2,1)S(1)}, u32[]{:S(2)}, u32[]{:S(2)}) collective-permute-start(bf16[64,2048]{1,0:T(8,128)(2,1)S(1)} %collective-permute-done.2.refs_4_), channel_id=1, source_target_pairs={{0,4},{4,0},{8,12},{12,8},{16,20},{20,16},{24,28},{28,24},{1,5},{5... | collective-permute-start | bytes 786440 | tf_op jit(solution)/shard_map/ppermute | solution.py:17
  25.8 8.8 %collective-permute-start.6 = (bf16[32,2048]{1,0:T(8,128)(2,1)S(1)}, bf16[32,2048]{1,0:T(8,128)(2,1)S(1)}, u32[]{:S(2)}, u32[]{:S(2)}) collective-permute-start(bf16[32,2048]{1,0:T(8,128)(2,1)S(1)} %slice.6), channel_id=1, source_target_pairs={{0,16},{4,20},{8,24},{12,28},{16,0},{20,4},{24,8},{28,12},{1,17},{... | collective-permute-start | bytes 393224 | tf_op jit(solution)/shard_map/ppermute | solution.py:17
  27.2 9.1 %collective-permute-start.3 = (bf16[64,2048]{1,0:T(8,128)(2,1)S(1)}, bf16[64,2048]{1,0:T(8,128)(2,1)S(1)}, u32[]{:S(2)}, u32[]{:S(2)}) collective-permute-start(bf16[64,2048]{1,0:T(8,128)(2,1)S(1)} %copy-done), channel_id=1, source_target_pairs={{0,4},{4,0},{8,12},{12,8},{16,20},{20,16},{24,28},{28,24},{1,5},{5... | collective-permute-start | bytes 786440 | tf_op jit(solution)/shard_map/ppermute | solution.py:17
  27.8 7.5 %collective-permute-start.7 = (bf16[32,2048]{1,0:T(8,128)(2,1)S(1)}, bf16[32,2048]{1,0:T(8,128)(2,1)S(1)}, u32[]{:S(2)}, u32[]{:S(2)}) collective-permute-start(bf16[32,2048]{1,0:T(8,128)(2,1)S(1)} %slice.7), channel_id=1, source_target_pairs={{0,8},{4,12},{8,0},{12,4},{16,24},{20,28},{24,16},{28,20},{1,9},{5... | collective-permute-start | bytes 393224 | tf_op jit(solution)/shard_map/ppermute | solution.py:17
  34.6 1.7 %collective-permute-start.8 = (bf16[32,2048]{1,0:T(8,128)(2,1)S(1)}, bf16[32,2048]{1,0:T(8,128)(2,1)S(1)}, u32[]{:S(2)}, u32[]{:S(2)}) collective-permute-start(bf16[32,2048]{1,0:T(8,128)(2,1)S(1)} %collective-permute-done.6.refs_6_), channel_id=1, source_target_pairs={{0,4},{4,0},{8,12},{12,8},{16,20},{20,16},{24,28},{28,24},{1,5},{5... | collective-permute-start | bytes 393224 | tf_op jit(solution)/shard_map/ppermute | solution.py:17
  35.3 1.9 %collective-permute-start.9 = (bf16[32,2048]{1,0:T(8,128)(2,1)S(1)}, bf16[32,2048]{1,0:T(8,128)(2,1)S(1)}, u32[]{:S(2)}, u32[]{:S(2)}) collective-permute-start(bf16[32,2048]{1,0:T(8,128)(2,1)S(1)} %collective-permute-done.7.refs_7_), channel_id=1, source_target_pairs={{0,4},{4,0},{8,12},{12,8},{16,20},{20,16},{24,28},{28,24},{1,5},{5... | collective-permute-start | bytes 393224 | tf_op jit(solution)/shard_map/ppermute | solution.py:17
where the time goes:
time: 42.6 us; the launch traced here: 41.8 us
  starting transfers between devices  22 us (52%)
  Pallas kernels  9.98 us (23%)
  waiting for transfers between devices  9.67 us (23%)
    pallas_call x4, Pallas kernels, whole_call(): pl.pallas_call(kernel, out_shape=out_shape, in_specs=[pl.BlockSpec(memory...  9.98 us
    ppermute x9, starting transfers between devices, partner(): return lax.ppermute(value, axis, pairs)  8.07 us
    ppermute x9, waiting for transfers between devices, partner(): return lax.ppermute(value, axis, pairs)  6.57 us
    all_to_all x1, starting transfers between devices, blocked(): lax.all_to_all(packed, 'ctx', split_axis=0, concat_axis=0, tiled=True)  5.37 us
    all_to_all x1, starting transfers between devices, blocked(): lax.all_to_all(mixed.reshape(tp_count * ctx_count, group, tok), ('tp', 'c...  5.24 us
    ppermute x1, starting transfers between devices, blocked(): lax.ppermute(mirrored, 'tp', [(z, tp_count - 1 - z) for z in range(tp_cou...  3.32 us
    all_to_all x1, waiting for transfers between devices, blocked(): lax.all_to_all(mixed.reshape(tp_count * ctx_count, group, tok), ('tp', 'c...  3.09 us
  transfers between devices with their start and end apart: 12, of which 3 were waited for; matrix products, arithmetic and copies ran while one was open for 0% of the time, Pallas kernels for 15%

commit v1 on v0

--- a/solution.py
+++ b/solution.py
@@ -440,8 +440,8 @@
             for s in range(pieces):
                 ready_ref[first + m * pieces + s] = mixed[m * group : (m + 1) * group, s * tok : (s + 1) * tok]
         span = pl.ds(first, blocks // 2 * pieces)
-        for copy in range(out_hbm.shape[0]):
-            sends.append(pltpu.make_async_copy(ready_ref.at[span], out_hbm.at[copy, span], sems.at[part, copy]))
+        for copy in range(out_hbm.shape[1]):
+            sends.append(pltpu.make_async_copy(ready_ref.at[span], out_hbm.at[span, copy], sems.at[part, copy]))
             sends[-1].start()
     for send in sends:
         send.wait()
@@ -454,9 +454,11 @@
     position = lax.axis_index("ctx")
     even = pl.multiple_of(position % 2 * rows, rows)
     odd = pl.multiple_of((1 - position % 2) * rows, rows)
+    ctx_count, tp_count = mixed_ref.shape[:2]
+    mixed = jnp.concatenate([mixed_ref[i, z] for z in range(tp_count) for i in range(ctx_count)], axis=0)
     sends = []
     for half, half_refs in enumerate((w_refs[:4], w_refs[4:])):
-        total = mul(jnp.concatenate([w_ref[...] for w_ref in half_refs], axis=0), mixed_ref[...])
+        total = mul(jnp.concatenate([w_ref[...] for w_ref in half_refs], axis=0), mixed)
         for pair in range(2):
             place = 2 * half + pair
             held_ref[place, pl.ds(even, rows)] = total[pair * tile : pair * tile + rows]
@@ -543,7 +545,7 @@
     )
     mixed = whole_call(
         functools.partial(conv_kernel, poles),
-        (jax.ShapeDtypeStruct((tp_count, ctx_count, group, tok), jnp.bfloat16),),
+        (jax.ShapeDtypeStruct((ctx_count, tp_count, group, tok), jnp.bfloat16),),
         [
             pltpu.VMEM((2, blocks, group, 2 * block), jnp.float32),
             pltpu.VMEM((2, blocks * group, block), jnp.float32),
@@ -570,8 +572,8 @@
         w_blocks += [block, partner(block, "ctx", 0)]
     w_blocks += w_far + [partner(block, "ctx", 0) for block in w_far]
     every = lax.all_to_all(
-        mixed.reshape(tp_count * ctx_count, group, tok), ("tp", "ctx"), split_axis=0, concat_axis=0, tiled=True
-    ).reshape(channels, tok)
+        mixed.reshape(ctx_count * tp_count, group, tok), ("ctx", "tp"), split_axis=0, concat_axis=0, tiled=True
+    ).reshape(ctx_count, tp_count, group, tok)
     return whole_call(
         project_kernel,
         (jax.ShapeDtypeStruct((tok, rows * ctx_count), jnp.bfloat16),),

time: 42.6 us -> 42.2 us (level); the launches traced: 41.8 us -> 41.9 us
  waiting for transfers between devices: 9.67 us -> 10.5 us
  starting transfers between devices: 22 us -> 21.2 us
    ppermute x9, starting transfers between devices: 8.07 us -> 7.3 us  [partner(): return lax.ppermute(value, axis, pairs)]
    all_to_all x1, waiting for transfers between devices: 3.09 us -> 3.6 us  [blocked(): lax.all_to_all(mixed.reshape(ctx_count * tp_count, group, tok), ('ctx', '...]
  transfers between devices with their start and end apart: 12 -> 12, of which waited for: 3 -> 4; matrix products, arithmetic and copies ran while one was open for 0% -> 0% of each run, Pallas kernels for 15% -> 15%
where the time goes in v1:
time: 42.2 us; the launch traced here: 41.9 us
  starting transfers between devices  21.2 us (50%)
  waiting for transfers between devices  10.5 us (25%)
  Pallas kernels  10 us (24%)
    pallas_call x4, Pallas kernels, whole_call(): pl.pallas_call(kernel, out_shape=out_shape, in_specs=[pl.BlockSpec(memory...  10 us
    ppermute x9, starting transfers between devices, partner(): return lax.ppermute(value, axis, pairs)  7.3 us
    ppermute x9, waiting for transfers between devices, partner(): return lax.ppermute(value, axis, pairs)  6.92 us
    all_to_all x1, starting transfers between devices, blocked(): lax.all_to_all(packed, 'ctx', split_axis=0, concat_axis=0, tiled=True)  5.37 us
    all_to_all x1, starting transfers between devices, blocked(): lax.all_to_all(mixed.reshape(ctx_count * tp_count, group, tok), ('ctx', '...  5.23 us
    all_to_all x1, waiting for transfers between devices, blocked(): lax.all_to_all(mixed.reshape(ctx_count * tp_count, group, tok), ('ctx', '...  3.6 us
    ppermute x1, starting transfers between devices, blocked(): lax.ppermute(mirrored, 'tp', [(z, tp_count - 1 - z) for z in range(tp_cou...  3.32 us
  transfers between devices with their start and end apart: 12, of which 4 were waited for; matrix products, arithmetic and copies ran while one was open for 0% of the time, Pallas kernels for 15%

profile of v1, /device:TPU:1, one launch (start us, length us, event | category | flops | bytes accessed | tf_op | source)
XLA Modules:
  0.0 41.9 jit_solution(8901466564723420833)
XLA Ops:
  0.0 2.0 %shard_map.64 = (bf16[8,3,64,128]{3,2,1,0:T(8,128)(2,1)}, f32[64,128]{1,0:T(8,128)}, f32[64,128]{1,0:T(8,128)}) custom-call(bf16[128,512]{1,0:T(8,128)(2,1)} %gate_hbm.1, bf16[128,512]{1,0:T(8,128)(2,1)} %value_hbm.1, bf16[128,512]{1,0:T(8,128)(2,1)} %post_hbm.1, f32[32,512]{1,0:T(8,128)} %bitcast.9, f32[32,512]{1,0:T(8,128)} %bitcast.10), custom_call_target="tpu_custom_call" | custom-call | bytes 786432 | tf_op jit(solution)/shard_map/pallas_call | solution.py:475
  2.0 0.0 copy-start
  2.0 0.0 copy-start.2
  2.0 0.0 copy-start.1
  2.0 5.4 %all-to-all-start = ((bf16[8,3,64,128]{3,2,1,0:T(8,128)(2,1)}), bf16[8,3,64,128]{3,2,1,0:T(8,128)(2,1)S(1)}, u32[]{:S(2)}, u32[]{:S(2)}) async-start(bf16[8,3,64,128]{3,2,1,0:T(8,128)(2,1)} %get-tuple-element.16), calls=%async_computation | async-start | bytes 786432 | tf_op jit(solution)/shard_map/all_to_all | solution.py:527
  7.4 0.0 copy-done
  7.4 1.4 %collective-permute-start.1 = (bf16[64,2048]{1,0:T(8,128)(2,1)S(1)}, bf16[64,2048]{1,0:T(8,128)(2,1)S(1)}, u32[]{:S(2)}, u32[]{:S(2)}) collective-permute-start(bf16[64,2048]{1,0:T(8,128)(2,1)S(1)} %copy-done), channel_id=1, source_target_pairs={{0,8},{4,12},{8,0},{12,4},{16,24},{20,28},{24,16},{28,20},{1,9},{5... | collective-permute-start | bytes 786440 | tf_op jit(solution)/shard_map/ppermute | solution.py:17
  8.8 1.2 %collective-permute-start.2 = (bf16[64,2048]{1,0:T(8,128)(2,1)S(1)}, bf16[64,2048]{1,0:T(8,128)(2,1)S(1)}, u32[]{:S(2)}, u32[]{:S(2)}) collective-permute-start(bf16[64,2048]{1,0:T(8,128)(2,1)S(1)} %copy-done), channel_id=1, source_target_pairs={{0,16},{4,20},{8,24},{12,28},{16,0},{20,4},{24,8},{28,12},{1,17},{... | collective-permute-start | bytes 786440 | tf_op jit(solution)/shard_map/ppermute | solution.py:17
  10.0 0.0 copy-done.2
  10.0 3.3 %collective-permute-start = (f32[64,128]{1,0:T(8,128)S(1)}, f32[64,128]{1,0:T(8,128)S(1)}, u32[]{:S(2)}, u32[]{:S(2)}) collective-permute-start(f32[64,128]{1,0:T(8,128)S(1)} %copy-done.2), channel_id=1, source_target_pairs={{0,3},{1,2},{2,1},{3,0},{4,7},{5,6},{6,5},{7,4},{8,11},{9,10},{10,... | collective-permute-start | bytes 98312 | tf_op jit(solution)/shard_map/ppermute | solution.py:526
  13.3 0.0 copy-done.1
  13.3 2.5 %shard_map.65 = (f32[2,4,64,512]{3,2,1,0:T(8,128)S(1)}, bf16[2,256,512]{2,1,0:T(8,128)(2,1)S(1)}, bf16[2,512,256]{2,1,0:T(8,128)(2,1)S(1)}) custom-call(f32[64,128]{1,0:T(8,128)S(1)} %copy-done.1), custom_call_target="tpu_custom_call" | custom-call | flops 402653184 | bytes 1048576 | tf_op jit(solution)/shard_map/pallas_call | solution.py:475
  15.8 0.0 collective-permute-done.par_ref
  15.8 0.0 all-to-all-done.x_ref
  15.8 4.0 %shard_map.66 = bf16[8,4,64,128]{3,2,1,0:T(8,128)(2,1)} custom-call(bf16[8,3,64,128]{3,2,1,0:T(8,128)(2,1)S(1)} %all-to-all-done.x_ref, f32[2,4,64,512]{3,2,1,0:T(8,128)S(1)} %get-tuple-element.18.own_ref, f32[64,128]{1,0:T(8,128)S(1)} %collective-permute-done.par_ref, bf16[2,256,512]{2,1,0:T(8,128)(2,1)S(1)} %get-tuple-element.20.table_ref, ...), custom_call_target="tpu_custom_call" | custom-call | flops 1610612736 | bytes 2097152 | tf_op jit(solution)/shard_map/pallas_call | solution.py:475
  19.8 0.0 collective-permute-done.1.refs_2_
  19.8 0.0 collective-permute-done.2.refs_4_
  19.9 5.2 %all-to-all-start.1 = ((bf16[32,64,128]{2,1,0:T(8,128)(2,1)}), bf16[32,64,128]{2,1,0:T(8,128)(2,1)S(1)}, u32[]{:S(2)}, u32[]{:S(2)}) async-start(bf16[32,64,128]{2,1,0:T(8,128)(2,1)} %bitcast.4), calls=%async_computation.1 | async-start | bytes 1048576 | tf_op jit(solution)/shard_map/all_to_all | solution.py:574
  25.1 0.3 collective-permute-start.4
  25.5 0.3 collective-permute-start.5
  25.8 1.4 %collective-permute-start.6 = (bf16[32,2048]{1,0:T(8,128)(2,1)S(1)}, bf16[32,2048]{1,0:T(8,128)(2,1)S(1)}, u32[]{:S(2)}, u32[]{:S(2)}) collective-permute-start(bf16[32,2048]{1,0:T(8,128)(2,1)S(1)} %slice.6), channel_id=1, source_target_pairs={{0,16},{4,20},{8,24},{12,28},{16,0},{20,4},{24,8},{28,12},{1,17},{... | collective-permute-start | bytes 393224 | tf_op jit(solution)/shard_map/ppermute | solution.py:17
  27.2 0.6 %collective-permute-start.3 = (bf16[64,2048]{1,0:T(8,128)(2,1)S(1)}, bf16[64,2048]{1,0:T(8,128)(2,1)S(1)}, u32[]{:S(2)}, u32[]{:S(2)}) collective-permute-start(bf16[64,2048]{1,0:T(8,128)(2,1)S(1)} %copy-done), channel_id=1, source_target_pairs={{0,4},{4,0},{8,12},{12,8},{16,20},{20,16},{24,28},{28,24},{1,5},{5... | collective-permute-start | bytes 786440 | tf_op jit(solution)/shard_map/ppermute | solution.py:17
  27.8 1.2 %collective-permute-start.7 = (bf16[32,2048]{1,0:T(8,128)(2,1)S(1)}, bf16[32,2048]{1,0:T(8,128)(2,1)S(1)}, u32[]{:S(2)}, u32[]{:S(2)}) collective-permute-start(bf16[32,2048]{1,0:T(8,128)(2,1)S(1)} %slice.7), channel_id=1, source_target_pairs={{0,8},{4,12},{8,0},{12,4},{16,24},{20,28},{24,16},{28,20},{1,9},{5... | collective-permute-start | bytes 393224 | tf_op jit(solution)/shard_map/ppermute | solution.py:17
  29.0 5.6 %collective-permute-done.6.refs_6_ = bf16[32,2048]{1,0:T(8,128)(2,1)S(1)} collective-permute-done((bf16[32,2048]{1,0:T(8,128)(2,1)S(1)}, bf16[32,2048]{1,0:T(8,128)(2,1)S(1)}, u32[]{:S(2)}, u32[]{:S(2)}) %collective-permute-start.6) | collective-permute-done | bytes 131104 | tf_op jit(solution)/shard_map/ppermute | solution.py:17
  34.6 0.9 %collective-permute-start.8 = (bf16[32,2048]{1,0:T(8,128)(2,1)S(1)}, bf16[32,2048]{1,0:T(8,128)(2,1)S(1)}, u32[]{:S(2)}, u32[]{:S(2)}) collective-permute-start(bf16[32,2048]{1,0:T(8,128)(2,1)S(1)} %collective-permute-done.6.refs_6_), channel_id=1, source_target_pairs={{0,4},{4,0},{8,12},{12,8},{16,20},{20,16},{24,28},{28,24},{1,5},{5... | collective-permute-start | bytes 393224 | tf_op jit(solution)/shard_map/ppermute | solution.py:17
  35.4 0.0 collective-permute-done.7.refs_7_
  35.4 0.0 collective-permute-start.9
  35.4 0.0 collective-permute-done.4.refs_3_
  35.4 0.0 collective-permute-done.5.refs_5_
  35.5 0.0 collective-permute-done.3.refs_1_
  35.5 1.0 %collective-permute-done.8.refs_8_ = bf16[32,2048]{1,0:T(8,128)(2,1)S(1)} collective-permute-done((bf16[32,2048]{1,0:T(8,128)(2,1)S(1)}, bf16[32,2048]{1,0:T(8,128)(2,1)S(1)}, u32[]{:S(2)}, u32[]{:S(2)}) %collective-permute-start.8) | collective-permute-done | bytes 131104 | tf_op jit(solution)/shard_map/ppermute | solution.py:17
  36.4 0.4 collective-permute-done.9.refs_9_
  36.8 3.6 %all-to-all-done.1 = bf16[32,64,128]{2,1,0:T(8,128)(2,1)S(1)} async-done(((bf16[32,64,128]{2,1,0:T(8,128)(2,1)}), bf16[32,64,128]{2,1,0:T(8,128)(2,1)S(1)}, u32[]{:S(2)}, u32[]{:S(2)}) %all-to-all-start.1) | async-done | bytes 524320 | tf_op jit(solution)/shard_map/all_to_all | solution.py:574
  40.4 1.5 %shard_map.67 = bf16[128,512]{1,0:T(8,128)(2,1)} custom-call(bf16[8,4,64,128]{3,2,1,0:T(8,128)(2,1)S(1)} %bitcast.8, bf16[64,2048]{1,0:T(8,128)(2,1)S(1)} %copy-done, bf16[64,2048]{1,0:T(8,128)(2,1)S(1)} %collective-permute-done.3.refs_1_, bf16[64,2048]{1,0:T(8,128)(2,1)S(1)} %collective-permute-done.1.refs_2_, ...), custom_call_target="tpu_custom_call" | custom-call | flops 268435456 | bytes 2097152 | tf_op jit(solution)/shard_map/pallas_call | solution.py:475
  (2 shorter events, 0.0 us)
Async XLA Ops:
  2.0 5.4 %copy-start = (bf16[64,2048]{1,0:T(8,128)(2,1)S(1)}, bf16[64,2048]{1,0:T(8,128)(2,1)}, u32[]{:S(2)}) copy-start(bf16[64,2048]{1,0:T(8,128)(2,1)} %refs_0_) | copy-start | bytes 786436
  2.0 8.0 %copy-start.2 = (f32[64,128]{1,0:T(8,128)S(1)}, f32[64,128]{1,0:T(8,128)}, u32[]{:S(2)}) copy-start(f32[64,128]{1,0:T(8,128)} %get-tuple-element.19) | copy-start | bytes 98308
  2.0 11.3 %copy-start.1 = (f32[64,128]{1,0:T(8,128)S(1)}, f32[64,128]{1,0:T(8,128)}, u32[]{:S(2)}) copy-start(f32[64,128]{1,0:T(8,128)} %get-tuple-element.17.par_ref) | copy-start | bytes 98308
  2.0 13.8 %all-to-all-start = ((bf16[8,3,64,128]{3,2,1,0:T(8,128)(2,1)}), bf16[8,3,64,128]{3,2,1,0:T(8,128)(2,1)S(1)}, u32[]{:S(2)}, u32[]{:S(2)}) async-start(bf16[8,3,64,128]{3,2,1,0:T(8,128)(2,1)} %get-tuple-element.16), calls=%async_computation | async-start | bytes 786432 | tf_op jit(solution)/shard_map/all_to_all | solution.py:527
  7.4 12.4 %collective-permute-start.1 = (bf16[64,2048]{1,0:T(8,128)(2,1)S(1)}, bf16[64,2048]{1,0:T(8,128)(2,1)S(1)}, u32[]{:S(2)}, u32[]{:S(2)}) collective-permute-start(bf16[64,2048]{1,0:T(8,128)(2,1)S(1)} %copy-done), channel_id=1, source_target_pairs={{0,8},{4,12},{8,0},{12,4},{16,24},{20,28},{24,16},{28,20},{1,9},{5... | collective-permute-start | bytes 786440 | tf_op jit(solution)/shard_map/ppermute | solution.py:17
  8.8 11.0 %collective-permute-start.2 = (bf16[64,2048]{1,0:T(8,128)(2,1)S(1)}, bf16[64,2048]{1,0:T(8,128)(2,1)S(1)}, u32[]{:S(2)}, u32[]{:S(2)}) collective-permute-start(bf16[64,2048]{1,0:T(8,128)(2,1)S(1)} %copy-done), channel_id=1, source_target_pairs={{0,16},{4,20},{8,24},{12,28},{16,0},{20,4},{24,8},{28,12},{1,17},{... | collective-permute-start | bytes 786440 | tf_op jit(solution)/shard_map/ppermute | solution.py:17
  10.0 5.8 %collective-permute-start = (f32[64,128]{1,0:T(8,128)S(1)}, f32[64,128]{1,0:T(8,128)S(1)}, u32[]{:S(2)}, u32[]{:S(2)}) collective-permute-start(f32[64,128]{1,0:T(8,128)S(1)} %copy-done.2), channel_id=1, source_target_pairs={{0,3},{1,2},{2,1},{3,0},{4,7},{5,6},{6,5},{7,4},{8,11},{9,10},{10,... | collective-permute-start | bytes 98312 | tf_op jit(solution)/shard_map/ppermute | solution.py:526
  19.9 20.5 %all-to-all-start.1 = ((bf16[32,64,128]{2,1,0:T(8,128)(2,1)}), bf16[32,64,128]{2,1,0:T(8,128)(2,1)S(1)}, u32[]{:S(2)}, u32[]{:S(2)}) async-start(bf16[32,64,128]{2,1,0:T(8,128)(2,1)} %bitcast.4), calls=%async_computation.1 | async-start | bytes 1048576 | tf_op jit(solution)/shard_map/all_to_all | solution.py:574
  25.1 10.3 %collective-permute-start.4 = (bf16[64,2048]{1,0:T(8,128)(2,1)S(1)}, bf16[64,2048]{1,0:T(8,128)(2,1)S(1)}, u32[]{:S(2)}, u32[]{:S(2)}) collective-permute-start(bf16[64,2048]{1,0:T(8,128)(2,1)S(1)} %collective-permute-done.1.refs_2_), channel_id=1, source_target_pairs={{0,4},{4,0},{8,12},{12,8},{16,20},{20,16},{24,28},{28,24},{1,5},{5... | collective-permute-start | bytes 786440 | tf_op jit(solution)/shard_map/ppermute | solution.py:17
  25.5 10.0 %collective-permute-start.5 = (bf16[64,2048]{1,0:T(8,128)(2,1)S(1)}, bf16[64,2048]{1,0:T(8,128)(2,1)S(1)}, u32[]{:S(2)}, u32[]{:S(2)}) collective-permute-start(bf16[64,2048]{1,0:T(8,128)(2,1)S(1)} %collective-permute-done.2.refs_4_), channel_id=1, source_target_pairs={{0,4},{4,0},{8,12},{12,8},{16,20},{20,16},{24,28},{28,24},{1,5},{5... | collective-permute-start | bytes 786440 | tf_op jit(solution)/shard_map/ppermute | solution.py:17
  25.8 8.8 %collective-permute-start.6 = (bf16[32,2048]{1,0:T(8,128)(2,1)S(1)}, bf16[32,2048]{1,0:T(8,128)(2,1)S(1)}, u32[]{:S(2)}, u32[]{:S(2)}) collective-permute-start(bf16[32,2048]{1,0:T(8,128)(2,1)S(1)} %slice.6), channel_id=1, source_target_pairs={{0,16},{4,20},{8,24},{12,28},{16,0},{20,4},{24,8},{28,12},{1,17},{... | collective-permute-start | bytes 393224 | tf_op jit(solution)/shard_map/ppermute | solution.py:17
  27.2 8.3 %collective-permute-start.3 = (bf16[64,2048]{1,0:T(8,128)(2,1)S(1)}, bf16[64,2048]{1,0:T(8,128)(2,1)S(1)}, u32[]{:S(2)}, u32[]{:S(2)}) collective-permute-start(bf16[64,2048]{1,0:T(8,128)(2,1)S(1)} %copy-done), channel_id=1, source_target_pairs={{0,4},{4,0},{8,12},{12,8},{16,20},{20,16},{24,28},{28,24},{1,5},{5... | collective-permute-start | bytes 786440 | tf_op jit(solution)/shard_map/ppermute | solution.py:17
  27.8 7.6 %collective-permute-start.7 = (bf16[32,2048]{1,0:T(8,128)(2,1)S(1)}, bf16[32,2048]{1,0:T(8,128)(2,1)S(1)}, u32[]{:S(2)}, u32[]{:S(2)}) collective-permute-start(bf16[32,2048]{1,0:T(8,128)(2,1)S(1)} %slice.7), channel_id=1, source_target_pairs={{0,8},{4,12},{8,0},{12,4},{16,24},{20,28},{24,16},{28,20},{1,9},{5... | collective-permute-start | bytes 393224 | tf_op jit(solution)/shard_map/ppermute | solution.py:17
  34.6 1.9 %collective-permute-start.8 = (bf16[32,2048]{1,0:T(8,128)(2,1)S(1)}, bf16[32,2048]{1,0:T(8,128)(2,1)S(1)}, u32[]{:S(2)}, u32[]{:S(2)}) collective-permute-start(bf16[32,2048]{1,0:T(8,128)(2,1)S(1)} %collective-permute-done.6.refs_6_), channel_id=1, source_target_pairs={{0,4},{4,0},{8,12},{12,8},{16,20},{20,16},{24,28},{28,24},{1,5},{5... | collective-permute-start | bytes 393224 | tf_op jit(solution)/shard_map/ppermute | solution.py:17
  35.4 1.3 %collective-permute-start.9 = (bf16[32,2048]{1,0:T(8,128)(2,1)S(1)}, bf16[32,2048]{1,0:T(8,128)(2,1)S(1)}, u32[]{:S(2)}, u32[]{:S(2)}) collective-permute-start(bf16[32,2048]{1,0:T(8,128)(2,1)S(1)} %collective-permute-done.7.refs_7_), channel_id=1, source_target_pairs={{0,4},{4,0},{8,12},{12,8},{16,20},{20,16},{24,28},{28,24},{1,5},{5... | collective-permute-start | bytes 393224 | tf_op jit(solution)/shard_map/ppermute | solution.py:17

commit v2 on v1

--- a/solution.py
+++ b/solution.py
@@ -227,8 +227,23 @@
 
 
 def cycle(row_factor, col_factor, modulus):
-    angle = (row_factor * col_factor % modulus).astype(jnp.float32) * (2.0 * math.pi / modulus)
-    return jnp.cos(angle), jnp.sin(angle)
+    quarter = modulus // 4
+    turned = row_factor * col_factor + quarter // 2
+    quadrant = turned // quarter % 4
+    angle = (turned % quarter - quarter // 2).astype(jnp.float32) * (2.0 * math.pi / modulus)
+    square = angle * angle
+
+    def series(first):
+        total = jnp.zeros_like(square)
+        for power in range(first + 10, first, -2):
+            total = (total + (-1.0) ** ((power - first) // 2) / math.factorial(power)) * square
+        return total
+
+    cos = 1.0 + series(0)
+    sin = angle + angle * series(1)
+    odd = quadrant % 2 == 1
+    cos, sin = jnp.where(odd, sin, cos), jnp.where(odd, cos, sin)
+    return jnp.where((quadrant == 1) | (quadrant == 2), -cos, cos), jnp.where(quadrant >= 2, -sin, sin)
 
 
 def put_tables(table_ref, back_ref):
@@ -270,8 +285,8 @@
 
 
 def pack_kernel(
-    gate_hbm, value_hbm, post_hbm, decay_hbm, residue_hbm,
-    out_hbm, own_hbm, sent_hbm, held_ref, cut_ref, ready_ref, sems, out_sems,
+    gate_hbm, value_hbm, post_hbm, decay_hbm, residue_hbm, w_hbm,
+    out_hbm, own_hbm, sent_hbm, lower_hbm, upper_hbm, held_ref, cut_ref, w_ref, ready_ref, sems, out_sems,
 ):
     ctx_count, _, group, tok = out_hbm.shape
     width = gate_hbm.shape[1]
@@ -282,6 +297,8 @@
         columns = pl.ds(pl.multiple_of(index * group // tok * tok, tok), tok)
         pairs += [(decay_hbm.at[:, columns], cut_ref.at[place, :half]), (residue_hbm.at[:, columns], cut_ref.at[place, half:])]
     pairs += [(source, held_ref.at[place]) for place, source in enumerate((value_hbm, gate_hbm, post_hbm))]
+    lower = w_hbm.shape[0] // 2
+    pairs += [(w_hbm.at[:lower], w_ref.at[0]), (w_hbm.at[lower:], w_ref.at[1])]
     copies = [pltpu.make_async_copy(*pair, sems.at[place]) for place, pair in enumerate(pairs)]
     for copy in copies:
         copy.start()
@@ -291,13 +308,17 @@
         copies[2 * place + 1].wait()
         sends.append(pltpu.make_async_copy(cut_ref.at[place], target, out_sems.at[3 + place]))
         sends[-1].start()
-    for place, copy in enumerate(copies[4:]):
+    for place, copy in enumerate(copies[4:7]):
         copy.wait()
         for first in range(0, width, tok):
             turned = held_ref[place, :, first : first + tok].T
             for part in range(tok // group):
                 ready_ref[first // group + part, place] = turned[part * group : (part + 1) * group]
         sends.append(pltpu.make_async_copy(ready_ref.at[:, place], out_hbm.at[:, place], out_sems.at[place]))
+        sends[-1].start()
+    for place, target in enumerate((lower_hbm, upper_hbm)):
+        copies[7 + place].wait()
+        sends.append(pltpu.make_async_copy(w_ref.at[place], target, out_sems.at[5 + place]))
         sends[-1].start()
     for send in sends:
         send.wait()
@@ -349,26 +370,28 @@
 
 
 def filter_kernel(poles, par_ref, out_ref, table_ref, back_ref, time_ref, turned_ref):
-    group = out_ref.shape[2]
+    group = out_ref.shape[1]
     put_tables(table_ref, back_ref)
     turned_ref[...] = par_ref[...].T
     turned = turned_ref[pl.ds(pl.multiple_of(lax.axis_index("ctx") * group % turned_ref.shape[0], group), group)]
-    for index in range(2):
-        put_spectra(poles, index, turned, out_ref.at[index], time_ref.at[index], table_ref)
+    put_spectra(poles, 0, turned, out_ref, time_ref, table_ref)
 
 
 def conv_kernel(
-    poles, x_ref, own_ref, par_ref, table_ref, back_ref, out_hbm,
-    paired_ref, time_ref, turned_ref, spec_ref, high_ref, ready_ref, sems,
+    poles, x_ref, own_ref, own_par_ref, par_ref, table_ref, back_ref, out_hbm,
+    next_ref, paired_ref, time_ref, turned_ref, own_turned_ref, spec_ref, high_ref, ready_ref, sems,
 ):
     turned_ref[...] = par_ref[...].T
-    blocks, group, twice = own_ref.shape[1:]
+    blocks, group, twice = own_ref.shape
     block = twice // 2
     rows_all = blocks * group
     tall, wide = 16, 128
     pieces = x_ref.shape[0] // blocks
     first = (x_ref.shape[0] - 1 - lax.axis_index("ctx")) * group % turned_ref.shape[0]
     turned = mirror_rows(turned_ref[pl.ds(pl.multiple_of(first, group), group)])
+    own_turned_ref[...] = own_par_ref[...].T
+    first = lax.axis_index("ctx") * group % turned_ref.shape[0]
+    own_turned = own_turned_ref[pl.ds(pl.multiple_of(first, group), group)]
 
     def rows_of(position):
         return jnp.concatenate(
@@ -386,9 +409,9 @@
             data.append((spec_ref[rows, lane : lane + wide], spec_ref[rows, block + lane : block + lane + wide]))
         sums = [None] * blocks
         for lag in range(blocks):
-            h_ref = (own_ref, paired_ref)[side]
-            f_re = h_ref[index, lag, row : row + tall, lane : lane + wide]
-            f_im = h_ref[index, lag, row : row + tall, block + lane : block + lane + wide]
+            h_ref = paired_ref.at[index] if side else (own_ref, next_ref)[index]
+            f_re = h_ref[lag, row : row + tall, lane : lane + wide]
+            f_im = h_ref[lag, row : row + tall, block + lane : block + lane + wide]
             for m in range(blocks - lag):
                 target, (d_re, d_im) = (m + lag, data[m]) if side == 0 else (m, data[m + lag])
                 if side == 0:
@@ -423,6 +446,7 @@
             keep(side * rows_all, row, lane, times(0, side, 0, row, lane))
         gated.append(halves(gate * to_time(sides[side])))
     put_spectra(poles, 1, turned, paired_ref.at[1], time_ref.at[1], table_ref)
+    put_spectra(poles, 1, own_turned, next_ref, time_ref.at[2], table_ref)
     for side in range(2):
         spec_ref[sides[side]] = mul3(*gated[side], table_ref)
     for row, lane in chunks:
@@ -457,7 +481,7 @@
     ctx_count, tp_count = mixed_ref.shape[:2]
     mixed = jnp.concatenate([mixed_ref[i, z] for z in range(tp_count) for i in range(ctx_count)], axis=0)
     sends = []
-    for half, half_refs in enumerate((w_refs[:4], w_refs[4:])):
+    for half, half_refs in enumerate((w_refs[:6], w_refs[6:])):
         total = mul(jnp.concatenate([w_ref[...] for w_ref in half_refs], axis=0), mixed)
         for pair in range(2):
             place = 2 * half + pair
@@ -499,19 +523,22 @@
     rows, channels = w_out.shape
     half = 2 * poles
 
-    packed, own, mirrored = whole_call(
+    packed, own, mirrored, w_lower, w_upper = whole_call(
         pack_kernel,
         (
             jax.ShapeDtypeStruct((ctx_count, 3, group, tok), jnp.bfloat16),
             jax.ShapeDtypeStruct((2 * half, tok), jnp.float32),
             jax.ShapeDtypeStruct((2 * half, tok), jnp.float32),
+            jax.ShapeDtypeStruct((rows // 2, channels), jnp.bfloat16),
+            jax.ShapeDtypeStruct((rows // 2, channels), jnp.bfloat16),
         ),
         [
             pltpu.VMEM((3, tok, width), jnp.bfloat16),
             pltpu.VMEM((2, 2 * half, tok), jnp.float32),
+            pltpu.VMEM((2, rows // 2, channels), jnp.bfloat16),
             pltpu.VMEM((ctx_count, 3, group, tok), jnp.bfloat16),
+            pltpu.SemaphoreType.DMA((9,)),
             pltpu.SemaphoreType.DMA((7,)),
-            pltpu.SemaphoreType.DMA((5,)),
         ],
         0,
         6 * tok * width * 2,
@@ -520,57 +547,62 @@
         x_post,
         jnp.swapaxes(decay, 1, 2).reshape(half, width),
         jnp.swapaxes(residue, 1, 2).reshape(half, width),
-        in_hbm=5,
-        out_hbm=(0, 1, 2),
+        w_out,
+        in_hbm=6,
+        out_hbm=(0, 1, 2, 3, 4),
     )
     paired = lax.ppermute(mirrored, "tp", [(z, tp_count - 1 - z) for z in range(tp_count)])
     received = lax.all_to_all(packed, "ctx", split_axis=0, concat_axis=0, tiled=True)
 
-    w_late, mirrored = lax.optimization_barrier((w_out, mirrored))
-    w_x, w_y = partner(w_late, "ctx", 1), partner(w_late, "ctx", 2)
+    w_x, w_y = partner(w_lower, "ctx", 1), partner(w_upper, "ctx", 2)
     own_spectra, table, back_table = whole_call(
         functools.partial(filter_kernel, poles),
         (
-            jax.ShapeDtypeStruct((2, blocks, group, 2 * block), jnp.float32),
+            jax.ShapeDtypeStruct((blocks, group, 2 * block), jnp.float32),
             jax.ShapeDtypeStruct((2, block, 2 * block), jnp.bfloat16),
             jax.ShapeDtypeStruct((2, 2 * block, block), jnp.bfloat16),
         ),
         [
-            pltpu.VMEM((2, blocks * group, block), jnp.float32),
+            pltpu.VMEM((blocks * group, block), jnp.float32),
             pltpu.VMEM((tok, 2 * half), jnp.float32),
         ],
-        2 * 2 * blocks * group * block * 2 * block * 3,
-        2 * blocks * group * 2 * block * 4,
+        2 * blocks * group * block * 2 * block * 3,
+        blocks * group * 2 * block * 4,
         own,
     )
     mixed = whole_call(
         functools.partial(conv_kernel, poles),
         (jax.ShapeDtypeStruct((ctx_count, tp_count, group, tok), jnp.bfloat16),),
         [
+            pltpu.VMEM((blocks, group, 2 * block), jnp.float32),
             pltpu.VMEM((2, blocks, group, 2 * block), jnp.float32),
-            pltpu.VMEM((2, blocks * group, block), jnp.float32),
+            pltpu.VMEM((3, blocks * group, block), jnp.float32),
+            pltpu.VMEM((tok, 2 * half), jnp.float32),
             pltpu.VMEM((tok, 2 * half), jnp.float32),
             pltpu.VMEM((2 * blocks * group, 2 * block), jnp.float32),
             pltpu.VMEM((2 * blocks * group, 2 * block), jnp.bfloat16),
             pltpu.VMEM((ctx_count, group, tok), jnp.bfloat16),
             pltpu.SemaphoreType.DMA((2, tp_count)),
         ],
-        2 * 8 * blocks * group * block * 2 * block * 3,
+        2 * 9 * blocks * group * block * 2 * block * 3,
         4 * blocks * group * 2 * block * 4,
         received,
         own_spectra,
+        own,
         paired,
         table,
         back_table,
         out_hbm=(0,),
     )
-    mixed, w_x, w_y, w_own = lax.optimization_barrier((mixed, w_x, w_y, w_out))
-    lower = rows // 2
-    w_far = [partner(w_x[:lower], "ctx", 2), partner(w_y[lower:], "ctx", 1)]
+    mixed, w_x, w_y, w_own, w_lower, w_upper = lax.optimization_barrier((mixed, w_x, w_y, w_out, w_lower, w_upper))
     w_blocks = []
-    for block in (w_own, w_x, w_y):
-        w_blocks += [block, partner(block, "ctx", 0)]
-    w_blocks += w_far + [partner(block, "ctx", 0) for block in w_far]
+    for block in (
+        [w_own],
+        [w_x, partner(w_upper, "ctx", 1)],
+        [partner(w_lower, "ctx", 2), w_y],
+        [partner(w_x, "ctx", 2), partner(w_y, "ctx", 1)],
+    ):
+        w_blocks += block + [partner(part, "ctx", 0) for part in block]
     every = lax.all_to_all(
         mixed.reshape(ctx_count * tp_count, group, tok), ("ctx", "tp"), split_axis=0, concat_axis=0, tiled=True
     ).reshape(ctx_count, tp_count, group, tok)

time: 42.2 us -> 45.2 us (1.071)
  starting transfers between devices: 21.2 us -> 25.3 us
  waiting for transfers between devices: 10.5 us -> 8.56 us
  Pallas kernels: 10 us -> 10.5 us
    ppermute x9 -> x13, starting transfers between devices: 7.3 us -> 11.9 us  [partner(): return lax.ppermute(value, axis, pairs)]
    all_to_all x1, waiting for transfers between devices: 3.6 us -> 0.01 us  [blocked(): lax.all_to_all(mixed.reshape(ctx_count * tp_count, group, tok), ('ctx', '...]
    ppermute x9 -> x13, waiting for transfers between devices: 6.92 us -> 8.56 us  [partner(): return lax.ppermute(value, axis, pairs)]
    pallas_call x4, Pallas kernels: 10 us -> 10.5 us  [whole_call(): pl.pallas_call(kernel, out_shape=out_shape, in_specs=[pl.BlockSpec(memory...]
  transfers between devices with their start and end apart: 12 -> 16, of which waited for: 4 -> 4; matrix products, arithmetic and copies ran while one was open for 0% -> 0% of each run, Pallas kernels for 15% -> 15%
where the time goes in v2:
time: 45.2 us; the launch traced here: 44.6 us
  starting transfers between devices  25.3 us (56%)
  Pallas kernels  10.5 us (23%)
  waiting for transfers between devices  8.56 us (19%)
    ppermute x13, starting transfers between devices, partner(): return lax.ppermute(value, axis, pairs)  11.9 us
    pallas_call x4, Pallas kernels, whole_call(): pl.pallas_call(kernel, out_shape=out_shape, in_specs=[pl.BlockSpec(memory...  10.5 us
    ppermute x13, waiting for transfers between devices, partner(): return lax.ppermute(value, axis, pairs)  8.56 us
    all_to_all x1, starting transfers between devices, blocked(): lax.all_to_all(packed, 'ctx', split_axis=0, concat_axis=0, tiled=True)  5.37 us
    all_to_all x1, starting transfers between devices, blocked(): lax.all_to_all(mixed.reshape(ctx_count * tp_count, group, tok), ('ctx', '...  4.79 us
    ppermute x1, starting transfers between devices, blocked(): lax.ppermute(mirrored, 'tp', [(z, tp_count - 1 - z) for z in range(tp_cou...  3.32 us
  transfers between devices with their start and end apart: 16, of which 4 were waited for; matrix products, arithmetic and copies ran while one was open for 0% of the time, Pallas kernels for 15%

profile of v2, /device:TPU:1, one launch (start us, length us, event | category | flops | bytes accessed | tf_op | source)
XLA Modules:
  0.0 44.6 jit_solution(1739893991150119364)
XLA Ops:
  0.0 2.1 %shard_map.64 = (bf16[8,3,64,128]{3,2,1,0:T(8,128)(2,1)}, f32[64,128]{1,0:T(8,128)}, f32[64,128]{1,0:T(8,128)}, bf16[32,2048]{1,0:T(8,128)(2,1)}, bf16[32,2048]{1,0:T(8,128)(2,1)}) custom-call(bf16[128,512]{1,0:T(8,128)(2,1)} %gate_hbm.1, bf16[128,512]{1,0:T(8,128)(2,1)} %value_hbm.1, bf16[128,512]{1,0:T(8,128)(2,1)} %post_hbm.1, f32[32,512]{1,0:T(8,128)} %bitcast.9, ...), custom_call_target="tpu_custom_call" | custom-call | bytes 786432 | tf_op jit(solution)/shard_map/pallas_call | solution.py:499
  2.1 0.0 copy-start.4
  2.1 0.0 copy-start.2
  2.2 0.0 copy-start.3
  2.2 0.0 copy-start.1
  2.2 5.4 %all-to-all-start = ((bf16[8,3,64,128]{3,2,1,0:T(8,128)(2,1)}), bf16[8,3,64,128]{3,2,1,0:T(8,128)(2,1)S(1)}, u32[]{:S(2)}, u32[]{:S(2)}) async-start(bf16[8,3,64,128]{3,2,1,0:T(8,128)(2,1)} %get-tuple-element.19), calls=%async_computation | async-start | bytes 786432 | tf_op jit(solution)/shard_map/all_to_all | solution.py:555
  7.5 0.0 copy-done.4
  7.5 3.3 %collective-permute-start = (f32[64,128]{1,0:T(8,128)S(1)}, f32[64,128]{1,0:T(8,128)S(1)}, u32[]{:S(2)}, u32[]{:S(2)}) collective-permute-start(f32[64,128]{1,0:T(8,128)S(1)} %copy-done.4), channel_id=1, source_target_pairs={{0,3},{1,2},{2,1},{3,0},{4,7},{5,6},{6,5},{7,4},{8,11},{9,10},{10,... | collective-permute-start | bytes 98312 | tf_op jit(solution)/shard_map/ppermute | solution.py:554
  10.9 0.0 copy-done.2
  10.9 1.4 %collective-permute-start.1 = (bf16[32,2048]{1,0:T(8,128)(2,1)S(1)}, bf16[32,2048]{1,0:T(8,128)(2,1)S(1)}, u32[]{:S(2)}, u32[]{:S(2)}) collective-permute-start(bf16[32,2048]{1,0:T(8,128)(2,1)S(1)} %copy-done.2), channel_id=1, source_target_pairs={{0,8},{4,12},{8,0},{12,4},{16,24},{20,28},{24,16},{28,20},{1,9},{5... | collective-permute-start | bytes 393224 | tf_op jit(solution)/shard_map/ppermute | solution.py:17
  12.3 0.0 copy-done.3
  12.3 1.2 %collective-permute-start.2 = (bf16[32,2048]{1,0:T(8,128)(2,1)S(1)}, bf16[32,2048]{1,0:T(8,128)(2,1)S(1)}, u32[]{:S(2)}, u32[]{:S(2)}) collective-permute-start(bf16[32,2048]{1,0:T(8,128)(2,1)S(1)} %copy-done.3), channel_id=1, source_target_pairs={{0,16},{4,20},{8,24},{12,28},{16,0},{20,4},{24,8},{28,12},{1,17},{... | collective-permute-start | bytes 393224 | tf_op jit(solution)/shard_map/ppermute | solution.py:17
  13.4 0.0 copy-done.1
  13.4 1.8 %shard_map.65 = (f32[4,64,512]{2,1,0:T(8,128)S(1)}, bf16[2,256,512]{2,1,0:T(8,128)(2,1)S(1)}, bf16[2,512,256]{2,1,0:T(8,128)(2,1)S(1)}) custom-call(f32[64,128]{1,0:T(8,128)S(1)} %copy-done.1), custom_call_target="tpu_custom_call" | custom-call | flops 201326592 | bytes 524288 | tf_op jit(solution)/shard_map/pallas_call | solution.py:499
  15.3 0.0 collective-permute-done.par_ref
  15.3 0.0 all-to-all-done.x_ref
  15.3 5.1 %shard_map.66 = bf16[8,4,64,128]{3,2,1,0:T(8,128)(2,1)} custom-call(bf16[8,3,64,128]{3,2,1,0:T(8,128)(2,1)S(1)} %all-to-all-done.x_ref, f32[4,64,512]{2,1,0:T(8,128)S(1)} %get-tuple-element.21.own_ref, f32[64,128]{1,0:T(8,128)S(1)} %copy-done.1, f32[64,128]{1,0:T(8,128)S(1)} %collective-permute-done.par_ref, ...), custom_call_target="tpu_custom_call" | custom-call | flops 1811939328 | bytes 2097152 | tf_op jit(solution)/shard_map/pallas_call | solution.py:499
  20.4 0.0 collective-permute-done.1.refs_2_
  20.4 0.0 collective-permute-done.2.refs_7_
  20.4 0.0 copy-start
  20.4 4.8 %all-to-all-start.1 = ((bf16[32,64,128]{2,1,0:T(8,128)(2,1)}), bf16[32,64,128]{2,1,0:T(8,128)(2,1)S(1)}, u32[]{:S(2)}, u32[]{:S(2)}) async-start(bf16[32,64,128]{2,1,0:T(8,128)(2,1)} %bitcast.4), calls=%async_computation.1 | async-start | bytes 1048576 | tf_op jit(solution)/shard_map/all_to_all | solution.py:606
  25.2 1.5 %collective-permute-start.4 = (bf16[32,2048]{1,0:T(8,128)(2,1)S(1)}, bf16[32,2048]{1,0:T(8,128)(2,1)S(1)}, u32[]{:S(2)}, u32[]{:S(2)}) collective-permute-start(bf16[32,2048]{1,0:T(8,128)(2,1)S(1)} %copy-done.3), channel_id=1, source_target_pairs={{0,8},{4,12},{8,0},{12,4},{16,24},{20,28},{24,16},{28,20},{1,9},{5... | collective-permute-start | bytes 393224 | tf_op jit(solution)/shard_map/ppermute | solution.py:17
  26.7 0.6 %collective-permute-start.5 = (bf16[32,2048]{1,0:T(8,128)(2,1)S(1)}, bf16[32,2048]{1,0:T(8,128)(2,1)S(1)}, u32[]{:S(2)}, u32[]{:S(2)}) collective-permute-start(bf16[32,2048]{1,0:T(8,128)(2,1)S(1)} %collective-permute-done.1.refs_2_), channel_id=1, source_target_pairs={{0,4},{4,0},{8,12},{12,8},{16,20},{20,16},{24,28},{28,24},{1,5},{5... | collective-permute-start | bytes 393224 | tf_op jit(solution)/shard_map/ppermute | solution.py:17
  27.3 0.0 copy-done
  27.3 0.0 collective-permute-start.3
  27.3 1.2 %collective-permute-start.7 = (bf16[32,2048]{1,0:T(8,128)(2,1)S(1)}, bf16[32,2048]{1,0:T(8,128)(2,1)S(1)}, u32[]{:S(2)}, u32[]{:S(2)}) collective-permute-start(bf16[32,2048]{1,0:T(8,128)(2,1)S(1)} %copy-done.2), channel_id=1, source_target_pairs={{0,16},{4,20},{8,24},{12,28},{16,0},{20,4},{24,8},{28,12},{1,17},{... | collective-permute-start | bytes 393224 | tf_op jit(solution)/shard_map/ppermute | solution.py:17
  28.5 0.8 %collective-permute-start.9 = (bf16[32,2048]{1,0:T(8,128)(2,1)S(1)}, bf16[32,2048]{1,0:T(8,128)(2,1)S(1)}, u32[]{:S(2)}, u32[]{:S(2)}) collective-permute-start(bf16[32,2048]{1,0:T(8,128)(2,1)S(1)} %collective-permute-done.2.refs_7_), channel_id=1, source_target_pairs={{0,4},{4,0},{8,12},{12,8},{16,20},{20,16},{24,28},{28,24},{1,5},{5... | collective-permute-start | bytes 393224 | tf_op jit(solution)/shard_map/ppermute | solution.py:17
  29.3 4.8 %collective-permute-done.4.refs_3_ = bf16[32,2048]{1,0:T(8,128)(2,1)S(1)} collective-permute-done((bf16[32,2048]{1,0:T(8,128)(2,1)S(1)}, bf16[32,2048]{1,0:T(8,128)(2,1)S(1)}, u32[]{:S(2)}, u32[]{:S(2)}) %collective-permute-start.4) | collective-permute-done | bytes 131104 | tf_op jit(solution)/shard_map/ppermute | solution.py:17
  34.1 1.2 %collective-permute-start.10 = (bf16[32,2048]{1,0:T(8,128)(2,1)S(1)}, bf16[32,2048]{1,0:T(8,128)(2,1)S(1)}, u32[]{:S(2)}, u32[]{:S(2)}) collective-permute-start(bf16[32,2048]{1,0:T(8,128)(2,1)S(1)} %collective-permute-done.1.refs_2_), channel_id=1, source_target_pairs={{0,16},{4,20},{8,24},{12,28},{16,0},{20,4},{24,8},{28,12},{1,17},{... | collective-permute-start | bytes 393224 | tf_op jit(solution)/shard_map/ppermute | solution.py:17
  35.3 0.0 collective-permute-done.5.refs_4_
  35.3 0.4 collective-permute-start.11
  35.8 0.0 collective-permute-done.7.refs_6_
  35.8 1.3 %collective-permute-start.6 = (bf16[32,2048]{1,0:T(8,128)(2,1)S(1)}, bf16[32,2048]{1,0:T(8,128)(2,1)S(1)}, u32[]{:S(2)}, u32[]{:S(2)}) collective-permute-start(bf16[32,2048]{1,0:T(8,128)(2,1)S(1)} %collective-permute-done.4.refs_3_), channel_id=1, source_target_pairs={{0,4},{4,0},{8,12},{12,8},{16,20},{20,16},{24,28},{28,24},{1,5},{5... | collective-permute-start | bytes 393224 | tf_op jit(solution)/shard_map/ppermute | solution.py:17
  37.0 0.0 collective-permute-done.9.refs_9_
  37.0 0.1 collective-permute-start.8
  37.1 2.7 %collective-permute-done.10.refs_10_ = bf16[32,2048]{1,0:T(8,128)(2,1)S(1)} collective-permute-done((bf16[32,2048]{1,0:T(8,128)(2,1)S(1)}, bf16[32,2048]{1,0:T(8,128)(2,1)S(1)}, u32[]{:S(2)}, u32[]{:S(2)}) %collective-permute-start.10) | collective-permute-done | bytes 131104 | tf_op jit(solution)/shard_map/ppermute | solution.py:17
  39.8 1.5 %collective-permute-start.12 = (bf16[32,2048]{1,0:T(8,128)(2,1)S(1)}, bf16[32,2048]{1,0:T(8,128)(2,1)S(1)}, u32[]{:S(2)}, u32[]{:S(2)}) collective-permute-start(bf16[32,2048]{1,0:T(8,128)(2,1)S(1)} %collective-permute-done.10.refs_10_), channel_id=1, source_target_pairs={{0,4},{4,0},{8,12},{12,8},{16,20},{20,16},{24,28},{28,24},{1,5},{5... | collective-permute-start | bytes 393224 | tf_op jit(solution)/shard_map/ppermute | solution.py:17
  41.3 0.0 collective-permute-done.11.refs_11_
  41.3 0.7 %collective-permute-start.13 = (bf16[32,2048]{1,0:T(8,128)(2,1)S(1)}, bf16[32,2048]{1,0:T(8,128)(2,1)S(1)}, u32[]{:S(2)}, u32[]{:S(2)}) collective-permute-start(bf16[32,2048]{1,0:T(8,128)(2,1)S(1)} %collective-permute-done.11.refs_11_), channel_id=1, source_target_pairs={{0,4},{4,0},{8,12},{12,8},{16,20},{20,16},{24,28},{28,24},{1,5},{5... | collective-permute-start | bytes 393224 | tf_op jit(solution)/shard_map/ppermute | solution.py:17
  42.1 0.0 collective-permute-done.3.refs_1_
  42.1 0.0 collective-permute-done.6.refs_5_
  42.1 0.0 collective-permute-done.8.refs_8_
  42.1 0.2 collective-permute-done.12.refs_12_
  42.3 0.7 %collective-permute-done.13.refs_13_ = bf16[32,2048]{1,0:T(8,128)(2,1)S(1)} collective-permute-done((bf16[32,2048]{1,0:T(8,128)(2,1)S(1)}, bf16[32,2048]{1,0:T(8,128)(2,1)S(1)}, u32[]{:S(2)}, u32[]{:S(2)}) %collective-permute-start.13) | collective-permute-done | bytes 131104 | tf_op jit(solution)/shard_map/ppermute | solution.py:17
  43.1 0.0 all-to-all-done.1
  43.1 1.5 %shard_map.67 = bf16[128,512]{1,0:T(8,128)(2,1)} custom-call(bf16[8,4,64,128]{3,2,1,0:T(8,128)(2,1)S(1)} %bitcast.8, bf16[64,2048]{1,0:T(8,128)(2,1)S(1)} %copy-done, bf16[64,2048]{1,0:T(8,128)(2,1)S(1)} %collective-permute-done.3.refs_1_, bf16[32,2048]{1,0:T(8,128)(2,1)S(1)} %collective-permute-done.1.refs_2_, ...), custom_call_target="tpu_custom_call" | custom-call | flops 268435456 | bytes 2097152 | tf_op jit(solution)/shard_map/pallas_call | solution.py:499
Async XLA Ops:
  2.1 5.4 %copy-start.4 = (f32[64,128]{1,0:T(8,128)S(1)}, f32[64,128]{1,0:T(8,128)}, u32[]{:S(2)}) copy-start(f32[64,128]{1,0:T(8,128)} %get-tuple-element.22) | copy-start | bytes 98308
  2.1 8.7 %copy-start.2 = (bf16[32,2048]{1,0:T(8,128)(2,1)S(1)}, bf16[32,2048]{1,0:T(8,128)(2,1)}, u32[]{:S(2)}) copy-start(bf16[32,2048]{1,0:T(8,128)(2,1)} %get-tuple-element.31) | copy-start | bytes 393220
  2.2 10.1 %copy-start.3 = (bf16[32,2048]{1,0:T(8,128)(2,1)S(1)}, bf16[32,2048]{1,0:T(8,128)(2,1)}, u32[]{:S(2)}) copy-start(bf16[32,2048]{1,0:T(8,128)(2,1)} %get-tuple-element.30) | copy-start | bytes 393220
  2.2 11.3 %copy-start.1 = (f32[64,128]{1,0:T(8,128)S(1)}, f32[64,128]{1,0:T(8,128)}, u32[]{:S(2)}) copy-start(f32[64,128]{1,0:T(8,128)} %get-tuple-element.20.par_ref.own_par_ref) | copy-start | bytes 98308
  2.2 13.1 %all-to-all-start = ((bf16[8,3,64,128]{3,2,1,0:T(8,128)(2,1)}), bf16[8,3,64,128]{3,2,1,0:T(8,128)(2,1)S(1)}, u32[]{:S(2)}, u32[]{:S(2)}) async-start(bf16[8,3,64,128]{3,2,1,0:T(8,128)(2,1)} %get-tuple-element.19), calls=%async_computation | async-start | bytes 786432 | tf_op jit(solution)/shard_map/all_to_all | solution.py:555
  7.5 7.7 %collective-permute-start = (f32[64,128]{1,0:T(8,128)S(1)}, f32[64,128]{1,0:T(8,128)S(1)}, u32[]{:S(2)}, u32[]{:S(2)}) collective-permute-start(f32[64,128]{1,0:T(8,128)S(1)} %copy-done.4), channel_id=1, source_target_pairs={{0,3},{1,2},{2,1},{3,0},{4,7},{5,6},{6,5},{7,4},{8,11},{9,10},{10,... | collective-permute-start | bytes 98312 | tf_op jit(solution)/shard_map/ppermute | solution.py:554
  10.9 9.5 %collective-permute-start.1 = (bf16[32,2048]{1,0:T(8,128)(2,1)S(1)}, bf16[32,2048]{1,0:T(8,128)(2,1)S(1)}, u32[]{:S(2)}, u32[]{:S(2)}) collective-permute-start(bf16[32,2048]{1,0:T(8,128)(2,1)S(1)} %copy-done.2), channel_id=1, source_target_pairs={{0,8},{4,12},{8,0},{12,4},{16,24},{20,28},{24,16},{28,20},{1,9},{5... | collective-permute-start | bytes 393224 | tf_op jit(solution)/shard_map/ppermute | solution.py:17
  12.3 8.1 %collective-permute-start.2 = (bf16[32,2048]{1,0:T(8,128)(2,1)S(1)}, bf16[32,2048]{1,0:T(8,128)(2,1)S(1)}, u32[]{:S(2)}, u32[]{:S(2)}) collective-permute-start(bf16[32,2048]{1,0:T(8,128)(2,1)S(1)} %copy-done.3), channel_id=1, source_target_pairs={{0,16},{4,20},{8,24},{12,28},{16,0},{20,4},{24,8},{28,12},{1,17},{... | collective-permute-start | bytes 393224 | tf_op jit(solution)/shard_map/ppermute | solution.py:17
  20.4 6.9 %copy-start = (bf16[64,2048]{1,0:T(8,128)(2,1)S(1)}, bf16[64,2048]{1,0:T(8,128)(2,1)}, u32[]{:S(2)}) copy-start(bf16[64,2048]{1,0:T(8,128)(2,1)} %refs_0_) | copy-start | bytes 786436
  20.4 22.7 %all-to-all-start.1 = ((bf16[32,64,128]{2,1,0:T(8,128)(2,1)}), bf16[32,64,128]{2,1,0:T(8,128)(2,1)S(1)}, u32[]{:S(2)}, u32[]{:S(2)}) async-start(bf16[32,64,128]{2,1,0:T(8,128)(2,1)} %bitcast.4), calls=%async_computation.1 | async-start | bytes 1048576 | tf_op jit(solution)/shard_map/all_to_all | solution.py:606
  25.2 8.9 %collective-permute-start.4 = (bf16[32,2048]{1,0:T(8,128)(2,1)S(1)}, bf16[32,2048]{1,0:T(8,128)(2,1)S(1)}, u32[]{:S(2)}, u32[]{:S(2)}) collective-permute-start(bf16[32,2048]{1,0:T(8,128)(2,1)S(1)} %copy-done.3), channel_id=1, source_target_pairs={{0,8},{4,12},{8,0},{12,4},{16,24},{20,28},{24,16},{28,20},{1,9},{5... | collective-permute-start | bytes 393224 | tf_op jit(solution)/shard_map/ppermute | solution.py:17
  26.7 8.7 %collective-permute-start.5 = (bf16[32,2048]{1,0:T(8,128)(2,1)S(1)}, bf16[32,2048]{1,0:T(8,128)(2,1)S(1)}, u32[]{:S(2)}, u32[]{:S(2)}) collective-permute-start(bf16[32,2048]{1,0:T(8,128)(2,1)S(1)} %collective-permute-done.1.refs_2_), channel_id=1, source_target_pairs={{0,4},{4,0},{8,12},{12,8},{16,20},{20,16},{24,28},{28,24},{1,5},{5... | collective-permute-start | bytes 393224 | tf_op jit(solution)/shard_map/ppermute | solution.py:17
  27.3 14.8 %collective-permute-start.3 = (bf16[64,2048]{1,0:T(8,128)(2,1)S(1)}, bf16[64,2048]{1,0:T(8,128)(2,1)S(1)}, u32[]{:S(2)}, u32[]{:S(2)}) collective-permute-start(bf16[64,2048]{1,0:T(8,128)(2,1)S(1)} %copy-done), channel_id=1, source_target_pairs={{0,4},{4,0},{8,12},{12,8},{16,20},{20,16},{24,28},{28,24},{1,5},{5... | collective-permute-start | bytes 786440 | tf_op jit(solution)/shard_map/ppermute | solution.py:17
  27.3 8.5 %collective-permute-start.7 = (bf16[32,2048]{1,0:T(8,128)(2,1)S(1)}, bf16[32,2048]{1,0:T(8,128)(2,1)S(1)}, u32[]{:S(2)}, u32[]{:S(2)}) collective-permute-start(bf16[32,2048]{1,0:T(8,128)(2,1)S(1)} %copy-done.2), channel_id=1, source_target_pairs={{0,16},{4,20},{8,24},{12,28},{16,0},{20,4},{24,8},{28,12},{1,17},{... | collective-permute-start | bytes 393224 | tf_op jit(solution)/shard_map/ppermute | solution.py:17
  28.5 8.5 %collective-permute-start.9 = (bf16[32,2048]{1,0:T(8,128)(2,1)S(1)}, bf16[32,2048]{1,0:T(8,128)(2,1)S(1)}, u32[]{:S(2)}, u32[]{:S(2)}) collective-permute-start(bf16[32,2048]{1,0:T(8,128)(2,1)S(1)} %collective-permute-done.2.refs_7_), channel_id=1, source_target_pairs={{0,4},{4,0},{8,12},{12,8},{16,20},{20,16},{24,28},{28,24},{1,5},{5... | collective-permute-start | bytes 393224 | tf_op jit(solution)/shard_map/ppermute | solution.py:17
  34.1 5.7 %collective-permute-start.10 = (bf16[32,2048]{1,0:T(8,128)(2,1)S(1)}, bf16[32,2048]{1,0:T(8,128)(2,1)S(1)}, u32[]{:S(2)}, u32[]{:S(2)}) collective-permute-start(bf16[32,2048]{1,0:T(8,128)(2,1)S(1)} %collective-permute-done.1.refs_2_), channel_id=1, source_target_pairs={{0,16},{4,20},{8,24},{12,28},{16,0},{20,4},{24,8},{28,12},{1,17},{... | collective-permute-start | bytes 393224 | tf_op jit(solution)/shard_map/ppermute | solution.py:17
  35.3 6.0 %collective-permute-start.11 = (bf16[32,2048]{1,0:T(8,128)(2,1)S(1)}, bf16[32,2048]{1,0:T(8,128)(2,1)S(1)}, u32[]{:S(2)}, u32[]{:S(2)}) collective-permute-start(bf16[32,2048]{1,0:T(8,128)(2,1)S(1)} %collective-permute-done.2.refs_7_), channel_id=1, source_target_pairs={{0,8},{4,12},{8,0},{12,4},{16,24},{20,28},{24,16},{28,20},{1,9},{5... | collective-permute-start | bytes 393224 | tf_op jit(solution)/shard_map/ppermute | solution.py:17
  35.8 6.3 %collective-permute-start.6 = (bf16[32,2048]{1,0:T(8,128)(2,1)S(1)}, bf16[32,2048]{1,0:T(8,128)(2,1)S(1)}, u32[]{:S(2)}, u32[]{:S(2)}) collective-permute-start(bf16[32,2048]{1,0:T(8,128)(2,1)S(1)} %collective-permute-done.4.refs_3_), channel_id=1, source_target_pairs={{0,4},{4,0},{8,12},{12,8},{16,20},{20,16},{24,28},{28,24},{1,5},{5... | collective-permute-start | bytes 393224 | tf_op jit(solution)/shard_map/ppermute | solution.py:17
  37.0 5.0 %collective-permute-start.8 = (bf16[32,2048]{1,0:T(8,128)(2,1)S(1)}, bf16[32,2048]{1,0:T(8,128)(2,1)S(1)}, u32[]{:S(2)}, u32[]{:S(2)}) collective-permute-start(bf16[32,2048]{1,0:T(8,128)(2,1)S(1)} %collective-permute-done.7.refs_6_), channel_id=1, source_target_pairs={{0,4},{4,0},{8,12},{12,8},{16,20},{20,16},{24,28},{28,24},{1,5},{5... | collective-permute-start | bytes 393224 | tf_op jit(solution)/shard_map/ppermute | solution.py:17
  39.8 2.5 %collective-permute-start.12 = (bf16[32,2048]{1,0:T(8,128)(2,1)S(1)}, bf16[32,2048]{1,0:T(8,128)(2,1)S(1)}, u32[]{:S(2)}, u32[]{:S(2)}) collective-permute-start(bf16[32,2048]{1,0:T(8,128)(2,1)S(1)} %collective-permute-done.10.refs_10_), channel_id=1, source_target_pairs={{0,4},{4,0},{8,12},{12,8},{16,20},{20,16},{24,28},{28,24},{1,5},{5... | collective-permute-start | bytes 393224 | tf_op jit(solution)/shard_map/ppermute | solution.py:17
  41.3 1.7 %collective-permute-start.13 = (bf16[32,2048]{1,0:T(8,128)(2,1)S(1)}, bf16[32,2048]{1,0:T(8,128)(2,1)S(1)}, u32[]{:S(2)}, u32[]{:S(2)}) collective-permute-start(bf16[32,2048]{1,0:T(8,128)(2,1)S(1)} %collective-permute-done.11.refs_11_), channel_id=1, source_target_pairs={{0,4},{4,0},{8,12},{12,8},{16,20},{20,16},{24,28},{28,24},{1,5},{5... | collective-permute-start | bytes 393224 | tf_op jit(solution)/shard_map/ppermute | solution.py:17
